TPU v7x, 128 devices: a whole 4x4x4 slice. The times are simulated.
128 devices in a mesh: ctx: 32 (over z_hi, y, x), head: 4 (over z_lo, core).
Axes of the slice: x: 4, y: 4, z: 4 (z_hi: 2, z_lo: 2; z = z_hi * 2 + z_lo), core: 2. Of those that a mesh axis runs over, the one named last changes fastest.
Arguments:
- queries: bfloat16 [16384, 16, 128], P('ctx', 'head'), may hold values from -15 to 15, as said below
- keys: bfloat16 [16384, 4, 128], P('ctx', 'head'), may hold values from -6 to 6, as said below
- values: bfloat16 [16384, 4, 128], P('ctx', 'head'), may hold values from -6 to 6
- out_weight: bfloat16 [2048, 4096], P('head'), may hold values from -0.5 to 0.5
Outputs:
- output: bfloat16 [16384, 4096], P('ctx', 'head')
Inputs may be any that keep to these rules, and one draw needn't show every extreme that they name: `queries`: dense real values. `keys`: dense real values.
All inputs are finite; a program needn't handle non-finite values.
Results may differ from a plain program's by a relative error of at most 0.015.
Values may be sent and summed in bfloat16 or wider, within the bound.
A program may use at most 64 MiB of HBM per device.

v0:
```python
import jax
import jax.numpy as jnp
from jax import lax
from jax.sharding import PartitionSpec as P

NEG_FILL = -1e30


def attend_block(state_in, query_half_rows, query_start_index, key_block, value_block, key_start):
    row_peak, row_total, accumulated = state_in
    query_rows = query_half_rows.shape[0]
    key_rows = key_block.shape[0]
    head_dim = query_half_rows.shape[-1]
    scores = jnp.einsum(
        "qhgd,khd->hgqk", query_half_rows, key_block, preferred_element_type=jnp.float32
    ) * head_dim ** (-0.5)
    query_pos = query_start_index + lax.iota(jnp.int32, query_rows)
    key_pos = key_start + lax.iota(jnp.int32, key_rows)
    allowed = key_pos[None, :] <= query_pos[:, None]
    scores = jnp.where(allowed, scores, NEG_FILL)
    new_peak = jnp.maximum(row_peak, jnp.max(scores, axis=-1))
    shrink = jnp.exp(row_peak - new_peak)
    weights = jnp.where(allowed, jnp.exp(scores - new_peak[..., None]), 0.0)
    new_total = row_total * shrink + jnp.sum(weights, axis=-1)
    update = jnp.einsum(
        "hgqk,khd->hgqd",
        weights.astype(jnp.bfloat16),
        value_block,
        preferred_element_type=jnp.float32,
    )
    return (new_peak, new_total, accumulated * shrink[..., None] + update)


def maybe_attend(state_in, query_half_rows, query_start_index, key_block, value_block, key_start):
    last_query = query_start_index + query_half_rows.shape[0] - 1
    return lax.cond(
        key_start <= last_query,
        lambda inner: attend_block(
            inner, query_half_rows, query_start_index, key_block, value_block, key_start
        ),
        lambda inner: inner,
        state_in,
    )


def finish_state(state_in, half_rows, query_heads, head_dim):
    row_peak, row_total, accumulated = state_in
    normed = accumulated / row_total[..., None]
    return (
        jnp.transpose(normed, (2, 0, 1, 3))
        .reshape(half_rows, query_heads * head_dim)
        .astype(jnp.bfloat16)
    )


def shards(queries, keys, values, out_weight):
    seq_rows, query_heads, head_dim = queries.shape
    key_heads = keys.shape[1]
    group_size = query_heads // key_heads
    half_rows = seq_rows // 2
    shard_index = lax.axis_index("ctx")
    shaped = queries.reshape(seq_rows, key_heads, group_size, head_dim)
    lower_rows = shaped[:half_rows]
    upper_rows = shaped[half_rows:]
    lower_start = shard_index * seq_rows
    upper_start = shard_index * seq_rows + half_rows
    initial = (
        jnp.full((key_heads, group_size, half_rows), NEG_FILL, jnp.float32),
        jnp.zeros((key_heads, group_size, half_rows), jnp.float32),
        jnp.zeros((key_heads, group_size, half_rows, head_dim), jnp.float32),
    )
    key_piece = lax.all_gather(keys, "ctx", axis=0, tiled=True)
    value_piece = lax.all_gather(values, "ctx", axis=0, tiled=True)
    block_count = key_piece.shape[0] // seq_rows
    key_blocks = key_piece.reshape(block_count, seq_rows, key_heads, head_dim)
    value_blocks = value_piece.reshape(block_count, seq_rows, key_heads, head_dim)
    block_starts = seq_rows * lax.iota(jnp.int32, block_count)

    def scan_step(pair_states, inputs):
        key_block, value_block, key_start = inputs
        lower_state = maybe_attend(
            pair_states[0], lower_rows, lower_start, key_block, value_block, key_start
        )
        upper_state = maybe_attend(
            pair_states[1], upper_rows, upper_start, key_block, value_block, key_start
        )
        return ((lower_state, upper_state), None)

    result_states, _ = lax.scan(
        scan_step, (initial, initial), (key_blocks, value_blocks, block_starts)
    )
    lower_state, upper_state = result_states
    lower_out = finish_state(lower_state, half_rows, query_heads, head_dim)
    upper_out = finish_state(upper_state, half_rows, query_heads, head_dim)
    attended = jnp.concatenate([lower_out, upper_out], axis=0)
    partial_sum = jnp.dot(attended, out_weight, preferred_element_type=jnp.float32)
    return lax.psum_scatter(
        partial_sum.astype(jnp.bfloat16), "head", scatter_dimension=1, tiled=True
    )


def solution(mesh):
    return jax.shard_map(
        shards,
        mesh=mesh,
        in_specs=(
            P("ctx", "head", None),
            P("ctx", "head", None),
            P("ctx", "head", None),
            P("head", None),
        ),
        out_specs=P("ctx", "head"),
        check_vma=False,
    )
```

profile of v0, /device:TPU:61, one launch (start us, length us, event | category | flops | bytes accessed | tf_op | source)
XLA Modules:
  0.0 510.0 jit_solution(15140009363212419281)
XLA Ops:
  8.1 1.2 fusion.42
  9.4 80.6 %all-gather.3.cloned.1.call-done = bf16[16384,1,128]{2,0,1:T(8,128)(2,1)} async-done(((bf16[512,1,128]{2,0,1:T(8,128)(2,1)}), bf16[16384,1,128]{2,0,1:T(8,128)(2,1)}) %all-gather.3.cloned.1.call-update) | async-done | bytes 4194320 | tf_op jit(solution)/shard_map/all_gather | solution.py:72
  89.9 82.3 %all-gather.5.cloned.1.call-done = bf16[16384,1,128]{2,0,1:T(8,128)(2,1)} async-done(((bf16[512,1,128]{2,0,1:T(8,128)(2,1)}), bf16[16384,1,128]{2,0,1:T(8,128)(2,1)}) %all-gather.5.cloned.1.call-update) | async-done | bytes 4194320 | tf_op jit(solution)/shard_map/all_gather | solution.py:73
  172.4 183.2 %while.23 = (s32[]{:T(128)}, f32[1,4,256]{2,1,0:T(4,128)S(1)}, f32[1,4,256]{2,1,0:T(4,128)S(1)}, f32[1,4,256,128]{3,2,1,0:T(8,128)S(1)}, f32[1,4,256]{2,1,0:T(4,...) while((s32[]{:T(128)}, f32[1,4,256]{2,1,0:T(4,128)S(1)}, ...), condition=%wide.region_9.10_spmd, body=%wide.region_0.9_spmd.sunk | while | flops 551296512 | bytes 17445320 | solution.py:89
  172.4 1.0 dynamic-slice_bitcast_fusion.3
  174.8 2.8 conditional.5
  178.3 2.8 conditional.4
  181.1 1.0 dynamic-slice_bitcast_fusion.3
  183.5 2.8 conditional.5
  187.0 2.8 conditional.4
  189.8 1.0 dynamic-slice_bitcast_fusion.3
  192.2 2.8 conditional.5
  195.7 2.8 conditional.4
  198.5 1.0 dynamic-slice_bitcast_fusion.3
  200.9 2.8 conditional.5
  204.4 2.8 conditional.4
  207.2 1.0 dynamic-slice_bitcast_fusion.3
  209.5 2.8 conditional.5
  213.0 2.8 conditional.4
  215.9 1.0 dynamic-slice_bitcast_fusion.3
  218.2 2.8 conditional.5
  221.7 2.8 conditional.4
  224.6 1.0 dynamic-slice_bitcast_fusion.3
  226.9 2.8 conditional.5
  230.4 2.8 conditional.4
  233.3 1.0 dynamic-slice_bitcast_fusion.3
  235.6 2.8 conditional.5
  239.1 2.8 conditional.4
  241.9 1.0 dynamic-slice_bitcast_fusion.3
  244.3 2.8 conditional.5
  247.8 2.8 conditional.4
  250.6 1.0 dynamic-slice_bitcast_fusion.3
  253.0 2.8 conditional.5
  256.5 2.8 conditional.4
  259.3 1.0 dynamic-slice_bitcast_fusion.3
  261.7 2.8 conditional.5
  265.2 2.8 conditional.4
  268.0 1.0 dynamic-slice_bitcast_fusion.3
  270.4 2.8 conditional.5
  273.9 2.8 conditional.4
  276.7 1.0 dynamic-slice_bitcast_fusion.3
  279.1 2.8 conditional.5
  282.6 2.8 conditional.4
  285.4 1.0 dynamic-slice_bitcast_fusion.3
  287.8 2.8 conditional.5
  291.3 2.8 conditional.4
  294.1 1.0 dynamic-slice_bitcast_fusion.3
  296.4 2.8 conditional.5
  299.9 2.8 conditional.4
  302.8 1.0 dynamic-slice_bitcast_fusion.3
  305.9 1.0 dynamic-slice_bitcast_fusion.3
  309.0 1.0 dynamic-slice_bitcast_fusion.3
  312.1 1.0 dynamic-slice_bitcast_fusion.3
  315.2 1.0 dynamic-slice_bitcast_fusion.3
  318.3 1.0 dynamic-slice_bitcast_fusion.3
  321.4 1.0 dynamic-slice_bitcast_fusion.3
  327.7 1.0 dynamic-slice_bitcast_fusion.3
  330.8 1.0 dynamic-slice_bitcast_fusion.3
  337.0 1.0 dynamic-slice_bitcast_fusion.3
  340.1 1.0 dynamic-slice_bitcast_fusion.3
  346.3 1.0 dynamic-slice_bitcast_fusion.3
  349.4 1.0 dynamic-slice_bitcast_fusion.3
  356.1 6.5 %convolution_convert_fusion = bf16[512,4096]{1,0:T(8,128)(2,1)} fusion(bf16[512,4096]{1,0:T(8,128)(2,1)} %param.13, bf16[256,512]{0,1:T(8,128)(2,1)S(1)} %bitcast.119, bf16[256,512]{0,1:T(8,128)(2,1)S(1)} %bitcast.118), kind=kOutput, calls=%fused_computation.56 | convolution fusion | flops 2150629376 | bytes 8912896 | tf_op jit(solution)/shard_map/dot_general | solution.py:96
  362.7 140.8 %reduce-scatter.2.cloned.1.call-done = bf16[512,1024]{1,0:T(8,128)(2,1)} async-done(((bf16[512,4096]{1,0:T(8,128)(2,1)}), bf16[512,1024]{1,0:T(8,128)(2,1)}) %reduce-scatter.2.cloned.1.call-update) | async-done | bytes 1048592 | tf_op jit(solution)/shard_map/reduce_scatter | solution.py:97
  (358 shorter events, 110.1 us)
Async XLA Ops:
  6.5 83.4 %all-gather.3.cloned.1.call-start = ((), (), s32[]{:S(2)}) async-start(), calls=%async_computation.1 | async-start | bytes 4325376 | tf_op jit(solution)/shard_map/all_gather | solution.py:72
  7.3 165.0 %all-gather.5.cloned.1.call-start = ((), (), s32[]{:S(2)}) async-start(), calls=%async_computation.2 | async-start | bytes 4325376 | tf_op jit(solution)/shard_map/all_gather | solution.py:73
  8.0 495.5 %reduce-scatter.2.cloned.1.call-start = ((), (), s32[]{:S(2)}) async-start(), calls=%async_computation.3 | async-start | bytes 5242880 | tf_op jit(solution)/shard_map/reduce_scatter | solution.py:97
Sparse Core Ops, SparseCore 0:
  10.3 79.5 all-gather.2
  92.9 79.3 all-gather.4
  362.8 140.6 reduce-scatter.1
where the time goes:
time: 515 us; the launch traced here: 510 us
  waiting for transfers between devices  305 us (59%)
  local copies, waits for them, and re-layouts  54.9 us (11%)
  loops' own time  48 us (9%)
  matrix products  46.8 us (9%)
  other arithmetic  41.9 us (8%)
  between operations  13.2 us (3%)
    reduce_scatter x1, waiting for transfers between devices, shards(): lax.psum_scatter(partial_sum.astype(jnp.bfloat16), 'head', scatter_dimens...  141 us
    all_gather x1, waiting for transfers between devices, shards(): value_piece = lax.all_gather(values, 'ctx', axis=0, tiled=True)  82.3 us
    all_gather x1, waiting for transfers between devices, shards(): key_piece = lax.all_gather(keys, 'ctx', axis=0, tiled=True)  80.6 us
    another operation x1, loops' own time, shards(): lax.scan(scan_step, (initial, initial), (key_blocks, value_blocks, block_...  45.6 us
    squeeze x32, local copies, waits for them, and re-layouts, shards(): lax.scan(scan_step, (initial, initial), (key_blocks, value_blocks, block_...  31.7 us
    dot_general x30, matrix products, attend_block(): jnp.einsum('hgqk,khd->hgqd', weights.astype(jnp.bfloat16), value_block, p...  25.9 us
    dynamic_slice x32, local copies, waits for them, and re-layouts, shards(): lax.scan(scan_step, (initial, initial), (key_blocks, value_blocks, block_...  21.3 us
    add x30, other arithmetic, attend_block(): key_pos = key_start + lax.iota(jnp.int32, key_rows)  20.7 us
  transfers between devices with their start and end apart: 3, of which 3 were waited for; matrix products, arithmetic and copies ran while one was open for 0% of the time, Pallas kernels for 0%

commit v1 on v0

v1 whole, which is shorter than its diff:
```python
import functools

import jax
import jax.numpy as jnp
from jax import lax
from jax.experimental import pallas as pl
from jax.experimental.pallas import tpu as pltpu
from jax.sharding import PartitionSpec as P

F32 = jnp.float32
BF16 = jnp.bfloat16
NEG = -1e30
SCALE = 128 ** -0.5 * 1.4426950408889634
FAR = 1 << 20
PAR_STEP = 5
TQ = 1024


def gray(n):
    return jnp.where(n == 2, 3, jnp.where(n == 3, 2, n))


def attend_kernel(
    q_ref, kv_ref, out_ref,
    kv, qb, acc, peak, o_send, o_recv, st_send, st_recv,
    send_sem, recv_sem, x_send, q_sem, o_sem, st_sem, local_sem,
):
    me = lax.axis_index("ctx")
    z, y, x = me // 16, (me // 4) % 4, me % 4
    place = me % 16
    other = 1 - z
    z_mate = other * 16 + place
    mate_place = 15 - place
    mate = other * 16 + mate_place

    def ctx(yy, xx):
        return z * 16 + ((yy + 4) % 4) * 4 + (xx + 4) % 4

    to_yp, to_ym, to_xp, to_xm = ctx(y + 1, x), ctx(y - 1, x), ctx(y, x + 1), ctx(y, x - 1)

    def slot(c, u, a):
        return (c * 2 + u) * 16 + a

    row = lax.broadcasted_iota(jnp.int32, (16, 128), 0)
    ones = jnp.where(row == 0, 1.0, 0.0).astype(BF16)

    @pl.loop(0, 64)
    def _(e):
        kv[e, pl.ds(256, 16), :] = ones

    own_copies = [
        pltpu.make_async_copy(
            kv_ref.at[z * 2 + u], kv.at[slot(z, u, place), pl.ds(0, 256)], local_sem.at[u]
        )
        for u in range(2)
    ]
    own_q = pltpu.make_async_copy(q_ref, qb.at[0], local_sem.at[2])
    for copy in own_copies:
        copy.start()
    own_q.start()

    barrier = pltpu.get_barrier_semaphore()
    for peer in (to_yp, to_ym, to_xp, to_xm, z_mate, mate):
        pl.semaphore_signal(barrier, inc=1, device_id={"ctx": peer}, device_id_type=pl.DeviceIdType.MESH)
    pl.semaphore_wait(barrier, 6)

    swaps = [
        pltpu.make_async_remote_copy(
            src_ref=kv_ref.at[other * 2 + u],
            dst_ref=kv.at[slot(z, u, place), pl.ds(0, 256)],
            send_sem=x_send.at[u],
            recv_sem=recv_sem.at[slot(z, u, place)],
            device_id={"ctx": z_mate},
            device_id_type=pl.DeviceIdType.MESH,
        )
        for u in range(2)
    ]
    for swap in swaps:
        swap.start()

    def relay(c, u, a, target, way):
        e = slot(c, u, a)
        return pltpu.make_async_remote_copy(
            src_ref=kv.at[e, pl.ds(0, 256)],
            dst_ref=kv.at[e, pl.ds(0, 256)],
            send_sem=send_sem.at[way, e],
            recv_sem=recv_sem.at[e],
            device_id={"ctx": target},
            device_id_type=pl.DeviceIdType.MESH,
        )

    def relays(c, u, a, first, second, act):
        if u == 0:
            p1, m1, p2, m2 = to_xp, to_xm, to_yp, to_ym
        else:
            p1, m1, p2, m2 = to_yp, to_ym, to_xp, to_xm
        line = second == 0
        conds = (
            (line | ((second == 3) & (c == 0)), p2),
            (line | ((second == 1) & (c == 1)), m2),
            (line & ((first == 0) | ((first == 3) & (c == 0))), p1),
            (line & ((first == 0) | ((first == 1) & (c == 1))), m1),
        )
        for way, (cond, target) in enumerate(conds):
            @pl.when(cond)
            def _():
                act(relay(c, u, a, target, way))

    def source(t, u):
        second, first = gray(t // 4), gray(t % 4)
        if u == 0:
            a = ((y + second) % 4) * 4 + (x + first) % 4
        else:
            a = ((y + first) % 4) * 4 + (x + second) % 4
        return a, first, second

    for copy in own_copies:
        copy.wait()
    for u in range(2):
        relays(z, u, place, 0 * place, 0 * place, lambda r: r.start())
    swap_q = pltpu.make_async_remote_copy(
        src_ref=q_ref, dst_ref=qb.at[1], send_sem=q_sem.at[0], recv_sem=q_sem.at[1],
        device_id={"ctx": mate}, device_id_type=pl.DeviceIdType.MESH,
    )
    swap_q.start()

    @pl.loop(0, 2)
    def _(n):
        acc[n] = jnp.zeros(acc.shape[1:], F32)
        peak[n] = jnp.full(peak.shape[1:], NEG, F32)

    own_q.wait()
    for u in range(2):
        relay(other, u, place, z_mate, 0).wait_recv()
    for u in range(2):
        relays(other, u, place, 0 * place, 0 * place, lambda r: r.start())

    def update(n, entries, bases):
        keys = jnp.concatenate([kv[e, pl.ds(0, 128), :] for e in entries], axis=0)
        vals = jnp.concatenate([kv[e, pl.ds(128, 144), :] for e in entries], axis=1)

        def scores(t):
            s = jnp.dot(keys, qb[n, :, pl.ds(t * TQ, TQ)], preferred_element_type=F32) * SCALE
            if bases is not None:
                k_at = lax.broadcasted_iota(jnp.int32, (128, TQ), 0)
                q_at = lax.broadcasted_iota(jnp.int32, (128, TQ), 1) % 512
                gap = q_at - k_at
                s = jnp.concatenate(
                    [jnp.where(gap >= b, s[i * 128:(i + 1) * 128], NEG) for i, b in enumerate(bases)], axis=0
                )
            return s

        def values(t, p, shrink):
            rows = pl.ds(t * TQ, TQ)
            acc[n, :, rows] = acc[n, :, rows] * shrink[:1] + jnp.dot(vals, p, preferred_element_type=F32)

        s = scores(0)
        held = None
        tiles = 2048 // TQ
        for t in range(tiles):
            after = scores(t + 1) if t + 1 < tiles else None
            rows = pl.ds(t * TQ, TQ)
            before = peak[n, :, rows]
            now = jnp.maximum(before, jnp.max(s, axis=0, keepdims=True))
            p = jnp.exp2(s - now[:1]).astype(BF16)
            peak[n, :, rows] = now
            if held is not None:
                values(*held)
            held = (t, p, jnp.exp2(before - now))
            s = after
        values(*held)

    kind = (z, other)
    at = (place, mate_place)

    def advance(n, state):
        t, count, *held = state
        for c in range(2):
            for u in range(2):
                a, _, _ = source(t, u)
                if c == 0:
                    ok = (kind[n] == 1) | (a < at[n])
                else:
                    ok = (kind[n] == 1) & (a < at[n])
                held = [jnp.where(ok & (count == k), slot(c, u, a), r) for k, r in enumerate(held)]
                count = count + ok.astype(jnp.int32)
        full = count >= 4

        @pl.when(full)
        def _():
            update(n, held[:4], None)

        held = [jnp.where(full, held[k + 4] if k < 3 else r, r) for k, r in enumerate(held)]
        return (t + 1, jnp.where(full, count - 4, count), *held)

    def finish(n, state):
        _, count, *held = state
        entries = [slot(kind[n], u, at[n]) for u in range(2)]
        bases = [z * 256 + u * 128 for u in range(2)]
        for k in range(3):
            there = k < count
            entries.append(jnp.where(there, held[k], slot(z, 0, place)))
            bases.append(jnp.where(there, -FAR, FAR))
        update(n, entries, bases)

    def step(t, carry):
        own, par = carry

        @pl.when(t > 0)
        def _():
            for u in range(2):
                a, first, second = source(t, u)
                for c in range(2):
                    relay(c, u, a, to_xp, 0).wait_recv()
                    relays(c, u, a, first, second, lambda r: r.start())

        @pl.when(t == PAR_STEP)
        def _():
            swap_q.wait_recv()

        n_par = jnp.where(t >= PAR_STEP, jnp.minimum(t + 1 - par[0], 2), 0)
        par = lax.fori_loop(0, n_par, lambda i, st: advance(1, st), par)
        n_own = jnp.minimum(t + 1 - own[0], jnp.where(n_par == 2, 0, 1))
        own = lax.fori_loop(0, n_own, lambda i, st: advance(0, st), own)
        return own, par

    zero = 0 * me
    start = (zero, zero) + (slot(z, 0, place),) * 7
    own, par = lax.fori_loop(0, 16, step, (start, start))
    par = lax.fori_loop(0, 16 - par[0], lambda i, st: advance(1, st), par)
    finish(1, par)

    for h in range(4):
        cols = pl.ds(h * 512, 512)
        o_send[:, cols] = acc[1, pl.ds(0, 128), cols].astype(BF16)
    st_send[pl.ds(0, 1), :] = peak[1, pl.ds(0, 1), :]
    st_send[pl.ds(1, 1), :] = acc[1, pl.ds(128, 1), :]
    swap_o = pltpu.make_async_remote_copy(
        src_ref=o_send, dst_ref=o_recv, send_sem=o_sem.at[0], recv_sem=o_sem.at[1],
        device_id={"ctx": mate}, device_id_type=pl.DeviceIdType.MESH,
    )
    swap_st = pltpu.make_async_remote_copy(
        src_ref=st_send, dst_ref=st_recv, send_sem=st_sem.at[0], recv_sem=st_sem.at[1],
        device_id={"ctx": mate}, device_id_type=pl.DeviceIdType.MESH,
    )
    swap_st.start()
    swap_o.start()

    own = lax.fori_loop(0, 16 - own[0], lambda i, st: advance(0, st), own)
    finish(0, own)

    swap_st.wait_recv()
    swap_o.wait_recv()
    for h in range(4):
        cols = pl.ds(h * 512, 512)
        mine, theirs = peak[0, pl.ds(0, 1), cols], st_recv[pl.ds(0, 1), cols]
        top = jnp.maximum(mine, theirs)
        a0, a1 = jnp.exp2(mine - top), jnp.exp2(theirs - top)
        total = acc[0, pl.ds(128, 1), cols] * a0 + st_recv[pl.ds(1, 1), cols] * a1
        mixed = acc[0, pl.ds(0, 128), cols] * a0 + o_recv[:, cols].astype(F32) * a1
        out_ref[pl.ds(h * 128, 128), :] = (mixed / total).astype(BF16)

    swap_st.wait_send()
    swap_o.wait_send()
    swap_q.wait_send()
    for swap in swaps:
        swap.wait_send()

    @pl.loop(0, 16)
    def _(t):
        for u in range(2):
            a, first, second = source(t, u)
            for c in range(2):
                relays(c, u, a, first, second, lambda r: r.wait_send())


def attend(q_t, kv_t):
    vmem = pl.BlockSpec(memory_space=pltpu.VMEM)
    return pl.pallas_call(
        attend_kernel,
        out_shape=jax.ShapeDtypeStruct((512, 512), BF16),
        in_specs=[vmem, vmem],
        out_specs=vmem,
        scratch_shapes=[
            pltpu.VMEM((64, 272, 128), BF16),
            pltpu.VMEM((2, 128, 2048), BF16),
            pltpu.VMEM((2, 144, 2048), F32),
            pltpu.VMEM((2, 8, 2048), F32),
            pltpu.VMEM((128, 2048), BF16),
            pltpu.VMEM((128, 2048), BF16),
            pltpu.VMEM((8, 2048), F32),
            pltpu.VMEM((8, 2048), F32),
                pltpu.SemaphoreType.DMA((4, 64)),
            pltpu.SemaphoreType.DMA((64,)),
            pltpu.SemaphoreType.DMA((2,)),
            pltpu.SemaphoreType.DMA((2,)),
            pltpu.SemaphoreType.DMA((2,)),
            pltpu.SemaphoreType.DMA((2,)),
            pltpu.SemaphoreType.DMA((3,)),
        ],
        compiler_params=pltpu.CompilerParams(
            collective_id=0, has_side_effects=True, vmem_limit_bytes=56 * 2 ** 20
        ),
    )(q_t, kv_t)


def shards(queries, keys, values, out_weight):
    q_t = queries.transpose(2, 1, 0).reshape(128, 2048)
    k_t = keys.reshape(4, 128, 128)
    v_t = values.reshape(4, 128, 128).transpose(0, 2, 1)
    kv_t = jnp.concatenate([k_t, v_t], axis=1)
    attended = attend(q_t, kv_t)
    partial_sum = lax.dot_general(attended, out_weight, (((0,), (0,)), ((), ())), preferred_element_type=F32)
    return lax.psum_scatter(partial_sum.astype(BF16), "head", scatter_dimension=1, tiled=True)


def solution(mesh):
    return jax.shard_map(
        shards,
        mesh=mesh,
        in_specs=(P("ctx", "head", None), P("ctx", "head", None), P("ctx", "head", None), P("head", None)),
        out_specs=P("ctx", "head"),
        check_vma=False,
    )
```

time: 515 us -> 154 us (0.30)
  waiting for transfers between devices: 305 us -> 49.9 us
  Pallas kernels: 0 us -> 76.4 us
  local copies, waits for them, and re-layouts: 54.9 us -> 3.46 us
  loops' own time: 48 us -> 0 us
  other arithmetic: 41.9 us -> 1.62 us
  matrix products: 46.8 us -> 6.67 us
    all_gather x2 -> x0, waiting for transfers between devices: 163 us -> none  [the longest x1 82.3 us: shards(): value_piece = lax.all_gather(values, 'ctx', axis=0, tiled=True)]
    reduce_scatter x1, waiting for transfers between devices: 141 us -> 49.8 us  [shards(): lax.psum_scatter(partial_sum.astype(BF16), 'head', scatter_dimension=1, t...]
    pallas_call x0 -> x1, Pallas kernels: none -> 76.4 us  [attend(): pl.pallas_call(attend_kernel, out_shape=jax.ShapeDtypeStruct((512, 512),...]
    another operation x65 -> x0, loops' own time: 48 us -> none  [the longest x1 45.6 us: shards(): lax.scan(scan_step, (initial, initial), (key_blocks, value_blocks, block_...]
    dot_general x61 -> x1, matrix products: 46.8 us -> 6.67 us  [shards(): lax.dot_general(attended, out_weight, (((0,), (0,)), ((), ())), preferred...]
    squeeze x32 -> x0, local copies, waits for them, and re-layouts: 31.7 us -> none  [shards(): lax.scan(scan_step, (initial, initial), (key_blocks, value_blocks, block_...]
    add x90 -> x0, other arithmetic: 21.4 us -> none  [the longest x30 20.7 us: attend_block(): key_pos = key_start + lax.iota(jnp.int32, key_rows)]
    dynamic_slice x32 -> x0, local copies, waits for them, and re-layouts: 21.3 us -> none  [shards(): lax.scan(scan_step, (initial, initial), (key_blocks, value_blocks, block_...]
  transfers between devices with their start and end apart: 3 -> 1, of which waited for: 3 -> 1; matrix products, arithmetic and copies ran while one was open for 0% -> 0% of each run, Pallas kernels for 0% -> 0%
where the time goes in v1:
time: 154 us; the launch traced here: 151 us
  Pallas kernels  76.4 us (50%)
  waiting for transfers between devices  49.9 us (32%)
  between operations  13.4 us (9%)
  matrix products  6.67 us (4%)
  local copies, waits for them, and re-layouts  3.46 us (2%)
  other arithmetic  1.62 us (1%)
    pallas_call x1, Pallas kernels, attend(): pl.pallas_call(attend_kernel, out_shape=jax.ShapeDtypeStruct((512, 512),...  76.4 us
    reduce_scatter x1, waiting for transfers between devices, shards(): lax.psum_scatter(partial_sum.astype(BF16), 'head', scatter_dimension=1, t...  49.8 us
    dot_general x1, matrix products, shards(): lax.dot_general(attended, out_weight, (((0,), (0,)), ((), ())), preferred...  6.67 us
  transfers between devices with their start and end apart: 1, of which 1 were waited for; matrix products, arithmetic and copies ran while one was open for 0% of the time, Pallas kernels for 0%

profile of v1, /device:TPU:61, one launch (start us, length us, event | category | flops | bytes accessed | tf_op | source)
XLA Modules:
  0.0 151.4 jit_solution(16450226228333243381)
XLA Ops:
  6.5 0.0 reduce-scatter.2.cloned.1.call-start
  6.5 1.0 copy.7
  7.6 1.5 %copy.6 = bf16[128,4,512]{2,1,0:T(4,128)(2,1)S(1)} copy(bf16[128,4,512]{0,1,2:T(4,128)(2,1)} %bitcast.10) | data formatting | bytes 1048576 | tf_op jit(solution)/shard_map/transpose | solution.py:308
  9.1 0.9 copy.8
  10.0 1.6 %pad_maximum_fusion.kv_ref = bf16[4,256,128]{2,1,0:T(8,128)(2,1)} fusion(bf16[4,128,128]{2,1,0:T(8,128)(2,1)S(1)} %bitcast.11, bf16[4,128,128]{2,1,0:T(8,128)(2,1)} %bitcast.13), kind=kLoop, calls=%fused_computation.1 | loop fusion | flops 524288 | bytes 524288 | tf_op jit(solution)/shard_map/concatenate | solution.py:311
  11.6 76.4 %shard_map.46 = bf16[512,512]{1,0:T(8,128)(2,1)} custom-call(bf16[128,2048]{1,0:T(8,128)(2,1)} %bitcast.8, bf16[4,256,128]{2,1,0:T(8,128)(2,1)} %pad_maximum_fusion.kv_ref), custom_call_target="tpu_custom_call" | custom-call | tf_op jit(solution)/shard_map/pallas_call | solution.py:279
  88.0 6.7 %convolution_convert_fusion = bf16[512,4096]{1,0:T(8,128)(2,1)} fusion(bf16[512,512]{1,0:T(8,128)(2,1)} %shard_map.46, bf16[512,4096]{1,0:T(8,128)(2,1)} %param.7), kind=kOutput, calls=%fused_computation | convolution fusion | flops 2149580800 | bytes 8912896 | tf_op jit(solution)/shard_map/dot_general | solution.py:313
  94.7 0.0 reduce-scatter.2.cloned.1.call-update
  94.7 49.8 %reduce-scatter.2.cloned.1.call-done = bf16[512,1024]{1,0:T(8,128)(2,1)} async-done(((bf16[512,4096]{1,0:T(8,128)(2,1)}), bf16[512,1024]{1,0:T(8,128)(2,1)}) %reduce-scatter.2.cloned.1.call-update) | async-done | bytes 1048592 | tf_op jit(solution)/shard_map/reduce_scatter | solution.py:314
Async XLA Ops:
  6.5 138.1 %reduce-scatter.2.cloned.1.call-start = ((), (), s32[]{:S(2)}) async-start(), calls=%async_computation.1 | async-start | bytes 5242880 | tf_op jit(solution)/shard_map/reduce_scatter | solution.py:314
Sparse Core Ops, SparseCore 0:
  94.9 49.6 reduce-scatter.1

commit v2 on v1

--- a/solution.py
+++ b/solution.py
@@ -12,6 +12,7 @@
 NEG = -1e30
 SCALE = 128 ** -0.5 * 1.4426950408889634
 FAR = 1 << 20
+W_LAG = 6
 PAR_STEP = 5
 TQ = 1024
 
@@ -21,9 +22,10 @@
 
 
 def attend_kernel(
-    q_ref, kv_ref, out_ref,
-    kv, qb, acc, peak, o_send, o_recv, st_send, st_recv,
+    q_ref, kv_ref, w_ref, out_ref,
+    kv, qb, acc, peak, o_send, o_recv, st_send, st_recv, w_all, att, total,
     send_sem, recv_sem, x_send, q_sem, o_sem, st_sem, local_sem,
+    w_send, w_recv, ws_send, wm_send, wm_recv, att_send, att_recv,
 ):
     me = lax.axis_index("ctx")
     z, y, x = me // 16, (me // 4) % 4, me % 4
@@ -32,6 +34,11 @@
     z_mate = other * 16 + place
     mate_place = 15 - place
     mate = other * 16 + mate_place
+    head = lax.axis_index("head")
+    core, zl = head % 2, head // 2
+    twin = zl * 2 + 1 - core
+    far = (1 - zl) * 2 + core
+    far_twin = (1 - zl) * 2 + 1 - core
 
     def ctx(yy, xx):
         return z * 16 + ((yy + 4) % 4) * 4 + (xx + 4) % 4
@@ -58,11 +65,19 @@
     for copy in own_copies:
         copy.start()
     own_q.start()
+    own_w = pltpu.make_async_copy(
+        w_ref.at[:, pl.ds(pl.multiple_of(head * 1024, 1024), 1024)],
+        w_all.at[pl.ds(pl.multiple_of(head * 512, 512), 512)],
+        local_sem.at[3],
+    )
+    own_w.start()
 
     barrier = pltpu.get_barrier_semaphore()
     for peer in (to_yp, to_ym, to_xp, to_xm, z_mate, mate):
         pl.semaphore_signal(barrier, inc=1, device_id={"ctx": peer}, device_id_type=pl.DeviceIdType.MESH)
-    pl.semaphore_wait(barrier, 6)
+    for peer in (twin, far, far_twin):
+        pl.semaphore_signal(barrier, inc=1, device_id={"head": peer}, device_id_type=pl.DeviceIdType.MESH)
+    pl.semaphore_wait(barrier, 9)
 
     swaps = [
         pltpu.make_async_remote_copy(
@@ -89,7 +104,40 @@
             device_id_type=pl.DeviceIdType.MESH,
         )
 
-    def relays(c, u, a, first, second, act):
+    def w_rows(c, u, a):
+        return pl.ds(pl.multiple_of(((1 - zl) * 2 + u) * 512 + a * 32 + c * 16, 16), 16)
+
+    def w_relay(c, u, a, target, way):
+        e = slot(c, u, a)
+        return pltpu.make_async_remote_copy(
+            src_ref=w_all.at[w_rows(c, u, a)],
+            dst_ref=w_all.at[w_rows(c, u, a)],
+            send_sem=w_send.at[way, e],
+            recv_sem=w_recv.at[e],
+            device_id={"ctx": target},
+            device_id_type=pl.DeviceIdType.MESH,
+        )
+
+    def w_slice(c, i, peer):
+        rows = place * 32 + c * 16
+        return pltpu.make_async_remote_copy(
+            src_ref=w_ref.at[pl.ds(pl.multiple_of(rows, 16), 16), pl.ds(pl.multiple_of(peer * 1024, 1024), 1024)],
+            dst_ref=w_all.at[pl.ds(pl.multiple_of(head * 512 + rows, 16), 16)],
+            send_sem=ws_send.at[i, c],
+            recv_sem=w_recv.at[slot(c, core, place)],
+            device_id={"head": peer},
+            device_id_type=pl.DeviceIdType.MESH,
+        )
+
+    w_slices = [w_slice(c, i, peer) for i, peer in enumerate((far, far_twin)) for c in range(2)]
+    w_twin = pltpu.make_async_remote_copy(
+        src_ref=w_ref.at[:, pl.ds(pl.multiple_of(twin * 1024, 1024), 1024)],
+        dst_ref=w_all.at[pl.ds(pl.multiple_of(head * 512, 512), 512)],
+        send_sem=wm_send, recv_sem=wm_recv,
+        device_id={"head": twin}, device_id_type=pl.DeviceIdType.MESH,
+    )
+
+    def relays(c, u, a, first, second, act, relay=relay):
         if u == 0:
             p1, m1, p2, m2 = to_xp, to_xm, to_yp, to_ym
         else:
@@ -123,6 +171,9 @@
         device_id={"ctx": mate}, device_id_type=pl.DeviceIdType.MESH,
     )
     swap_q.start()
+    for copy in w_slices:
+        copy.start()
+    w_twin.start()
 
     @pl.loop(0, 2)
     def _(n):
@@ -170,8 +221,11 @@
             s = after
         values(*held)
 
-    kind = (z, other)
-    at = (place, mate_place)
+    def kind_of(n):
+        return jnp.where(n == 0, z, other)
+
+    def at_of(n):
+        return jnp.where(n == 0, place, mate_place)
 
     def advance(n, state):
         t, count, *held = state
@@ -179,9 +233,9 @@
             for u in range(2):
                 a, _, _ = source(t, u)
                 if c == 0:
-                    ok = (kind[n] == 1) | (a < at[n])
+                    ok = (kind_of(n) == 1) | (a < at_of(n))
                 else:
-                    ok = (kind[n] == 1) & (a < at[n])
+                    ok = (kind_of(n) == 1) & (a < at_of(n))
                 held = [jnp.where(ok & (count == k), slot(c, u, a), r) for k, r in enumerate(held)]
                 count = count + ok.astype(jnp.int32)
         full = count >= 4
@@ -195,7 +249,7 @@
 
     def finish(n, state):
         _, count, *held = state
-        entries = [slot(kind[n], u, at[n]) for u in range(2)]
+        entries = [slot(kind_of(n), u, at_of(n)) for u in range(2)]
         bases = [z * 256 + u * 128 for u in range(2)]
         for k in range(3):
             there = k < count
@@ -203,10 +257,11 @@
             bases.append(jnp.where(there, -FAR, FAR))
         update(n, entries, bases)
 
+    def pick(n, yes, no):
+        return jnp.where(n == 1, yes, no)
+
     def step(t, carry):
-        own, par = carry
-
-        @pl.when(t > 0)
+        @pl.when((t > 0) & (t < 16))
         def _():
             for u in range(2):
                 a, first, second = source(t, u)
@@ -214,57 +269,134 @@
                     relay(c, u, a, to_xp, 0).wait_recv()
                     relays(c, u, a, first, second, lambda r: r.start())
 
+        @pl.when(t >= W_LAG)
+        def _():
+            for u in range(2):
+                a, first, second = source(t - W_LAG, u)
+                for c in range(2):
+                    w_relay(c, u, a, to_xp, 0).wait_recv()
+                    relays(c, u, a, first, second, lambda r: r.start(), w_relay)
+
         @pl.when(t == PAR_STEP)
         def _():
             swap_q.wait_recv()
 
-        n_par = jnp.where(t >= PAR_STEP, jnp.minimum(t + 1 - par[0], 2), 0)
-        par = lax.fori_loop(0, n_par, lambda i, st: advance(1, st), par)
-        n_own = jnp.minimum(t + 1 - own[0], jnp.where(n_par == 2, 0, 1))
-        own = lax.fori_loop(0, n_own, lambda i, st: advance(0, st), own)
-        return own, par
+        ready = jnp.minimum(t + 1, 16)
+
+        def one(i, carry):
+            own, par = carry
+            n = ((t >= PAR_STEP) & (par[0] < ready)).astype(jnp.int32)
+            state = advance(n, tuple(pick(n, p, o) for o, p in zip(own, par)))
+            return (
+                tuple(pick(n, o, v) for o, v in zip(own, state)),
+                tuple(pick(n, v, p) for p, v in zip(par, state)),
+            )
+
+        own, par = carry
+        open_own = ready - own[0]
+        open_par = jnp.where(t >= PAR_STEP, ready - par[0], 0)
+        return lax.fori_loop(0, jnp.minimum(open_own + open_par, 2), one, (own, par))
 
     zero = 0 * me
     start = (zero, zero) + (slot(z, 0, place),) * 7
-    own, par = lax.fori_loop(0, 16, step, (start, start))
-    par = lax.fori_loop(0, 16 - par[0], lambda i, st: advance(1, st), par)
-    finish(1, par)
-
-    for h in range(4):
-        cols = pl.ds(h * 512, 512)
-        o_send[:, cols] = acc[1, pl.ds(0, 128), cols].astype(BF16)
-    st_send[pl.ds(0, 1), :] = peak[1, pl.ds(0, 1), :]
-    st_send[pl.ds(1, 1), :] = acc[1, pl.ds(128, 1), :]
-    swap_o = pltpu.make_async_remote_copy(
-        src_ref=o_send, dst_ref=o_recv, send_sem=o_sem.at[0], recv_sem=o_sem.at[1],
-        device_id={"ctx": mate}, device_id_type=pl.DeviceIdType.MESH,
-    )
+    own, par = lax.fori_loop(0, 16 + W_LAG, step, (start, start))
+
+    def o_copy(i):
+        cols = pl.ds(i * 512, 512)
+        return pltpu.make_async_remote_copy(
+            src_ref=o_send.at[:, cols], dst_ref=o_recv.at[:, cols], send_sem=o_sem.at[0, i], recv_sem=o_sem.at[1, i],
+            device_id={"ctx": mate}, device_id_type=pl.DeviceIdType.MESH,
+        )
+
+    swap_o = [o_copy(i) for i in range(4)]
     swap_st = pltpu.make_async_remote_copy(
         src_ref=st_send, dst_ref=st_recv, send_sem=st_sem.at[0], recv_sem=st_sem.at[1],
         device_id={"ctx": mate}, device_id_type=pl.DeviceIdType.MESH,
     )
-    swap_st.start()
-    swap_o.start()
-
-    own = lax.fori_loop(0, 16 - own[0], lambda i, st: advance(0, st), own)
-    finish(0, own)
+
+    def close(j, carry):
+        n = 1 - j
+        state = tuple(pick(n, p, o) for o, p in zip(own, par))
+        state = lax.fori_loop(0, 16 - state[0], lambda i, st: advance(n, st), state)
+        finish(n, state)
+
+        @pl.when(j == 0)
+        def _():
+            st_send[pl.ds(0, 1), :] = peak[1, pl.ds(0, 1), :]
+            st_send[pl.ds(1, 1), :] = acc[1, pl.ds(128, 1), :]
+            swap_st.start()
+            for i in range(4):
+                cols = pl.ds(i * 512, 512)
+                o_send[:, cols] = acc[1, pl.ds(0, 128), cols].astype(BF16)
+                swap_o[i].start()
+
+        return carry
+
+    lax.fori_loop(0, 2, close, 0)
+
+    def att_copy(k, i, piece, peer):
+        return pltpu.make_async_remote_copy(
+            src_ref=att.at[piece], dst_ref=att.at[piece], send_sem=att_send.at[k, i], recv_sem=att_recv.at[piece],
+            device_id={"head": peer}, device_id_type=pl.DeviceIdType.MESH,
+        )
 
     swap_st.wait_recv()
-    swap_o.wait_recv()
-    for h in range(4):
-        cols = pl.ds(h * 512, 512)
+    for i in range(4):
+        swap_o[i].wait_recv()
+        cols = pl.ds(i * 512, 512)
         mine, theirs = peak[0, pl.ds(0, 1), cols], st_recv[pl.ds(0, 1), cols]
         top = jnp.maximum(mine, theirs)
         a0, a1 = jnp.exp2(mine - top), jnp.exp2(theirs - top)
-        total = acc[0, pl.ds(128, 1), cols] * a0 + st_recv[pl.ds(1, 1), cols] * a1
+        norm = acc[0, pl.ds(128, 1), cols] * a0 + st_recv[pl.ds(1, 1), cols] * a1
         mixed = acc[0, pl.ds(0, 128), cols] * a0 + o_recv[:, cols].astype(F32) * a1
-        out_ref[pl.ds(h * 128, 128), :] = (mixed / total).astype(BF16)
+        att[head * 4 + i] = (mixed / norm).T.astype(BF16)
+        att_copy(0, i, head * 4 + i, far).start()
+        att_copy(1, i, head * 4 + i, twin).start()
+
+    own_w.wait()
+    w_twin.wait_recv()
+
+    def project(g, carry):
+        h = jnp.where(g == 0, head, jnp.where(g == 1, twin, jnp.where(g == 2, far, far_twin)))
+
+        @pl.when(g > 0)
+        def _():
+            for i in range(4):
+                att_copy(0, i, h * 4 + i, twin).wait_recv()
+
+                @pl.when(g == 2)
+                def _():
+                    att_copy(2, i, h * 4 + i, twin).start()
+
+        left = jnp.concatenate([att[h * 4 + i] for i in range(4)], axis=1)
+        right = w_all[pl.ds(pl.multiple_of(h * 512, 512), 512), :]
+        term = jnp.dot(left, right, preferred_element_type=F32)
+
+        @pl.when(g == 0)
+        def _():
+            total[...] = term
+
+        @pl.when(g > 0)
+        def _():
+            total[...] += term
+
+        return carry
+
+    lax.fori_loop(0, 4, project, 0)
+    out_ref[...] = total[...].astype(BF16)
 
     swap_st.wait_send()
-    swap_o.wait_send()
+    for i in range(4):
+        swap_o[i].wait_send()
+        att_copy(0, i, head * 4 + i, far).wait_send()
+        att_copy(1, i, head * 4 + i, twin).wait_send()
+        att_copy(2, i, far * 4 + i, twin).wait_send()
     swap_q.wait_send()
     for swap in swaps:
         swap.wait_send()
+    for copy in w_slices:
+        copy.wait_send()
+    w_twin.wait_send()
 
     @pl.loop(0, 16)
     def _(t):
@@ -272,14 +404,15 @@
             a, first, second = source(t, u)
             for c in range(2):
                 relays(c, u, a, first, second, lambda r: r.wait_send())
-
-
-def attend(q_t, kv_t):
+                relays(c, u, a, first, second, lambda r: r.wait_send(), w_relay)
+
+
+def attend(q_t, kv_t, weight):
     vmem = pl.BlockSpec(memory_space=pltpu.VMEM)
     return pl.pallas_call(
         attend_kernel,
-        out_shape=jax.ShapeDtypeStruct((512, 512), BF16),
-        in_specs=[vmem, vmem],
+        out_shape=jax.ShapeDtypeStruct((512, 1024), BF16),
+        in_specs=[vmem, vmem, pl.BlockSpec(memory_space=pl.ANY)],
         out_specs=vmem,
         scratch_shapes=[
             pltpu.VMEM((64, 272, 128), BF16),
@@ -290,18 +423,28 @@
             pltpu.VMEM((128, 2048), BF16),
             pltpu.VMEM((8, 2048), F32),
             pltpu.VMEM((8, 2048), F32),
-                pltpu.SemaphoreType.DMA((4, 64)),
+            pltpu.VMEM((2048, 1024), BF16),
+            pltpu.VMEM((16, 512, 128), BF16),
+            pltpu.VMEM((512, 1024), F32),
+            pltpu.SemaphoreType.DMA((4, 64)),
             pltpu.SemaphoreType.DMA((64,)),
             pltpu.SemaphoreType.DMA((2,)),
             pltpu.SemaphoreType.DMA((2,)),
+            pltpu.SemaphoreType.DMA((2, 4)),
             pltpu.SemaphoreType.DMA((2,)),
-            pltpu.SemaphoreType.DMA((2,)),
-            pltpu.SemaphoreType.DMA((3,)),
+            pltpu.SemaphoreType.DMA((4,)),
+            pltpu.SemaphoreType.DMA((4, 64)),
+            pltpu.SemaphoreType.DMA((64,)),
+            pltpu.SemaphoreType.DMA((2, 2)),
+            pltpu.SemaphoreType.DMA,
+            pltpu.SemaphoreType.DMA,
+            pltpu.SemaphoreType.DMA((3, 4)),
+            pltpu.SemaphoreType.DMA((16,)),
         ],
         compiler_params=pltpu.CompilerParams(
             collective_id=0, has_side_effects=True, vmem_limit_bytes=56 * 2 ** 20
         ),
-    )(q_t, kv_t)
+    )(q_t, kv_t, weight)
 
 
 def shards(queries, keys, values, out_weight):
@@ -309,9 +452,7 @@
     k_t = keys.reshape(4, 128, 128)
     v_t = values.reshape(4, 128, 128).transpose(0, 2, 1)
     kv_t = jnp.concatenate([k_t, v_t], axis=1)
-    attended = attend(q_t, kv_t)
-    partial_sum = lax.dot_general(attended, out_weight, (((0,), (0,)), ((), ())), preferred_element_type=F32)
-    return lax.psum_scatter(partial_sum.astype(BF16), "head", scatter_dimension=1, tiled=True)
+    return attend(q_t, kv_t, out_weight)
 
 
 def solution(mesh):

time: 154 us -> 120 us (0.78); the launches traced: 151 us -> 120 us
  waiting for transfers between devices: 49.9 us -> 0 us
  Pallas kernels: 76.4 us -> 113 us
  between operations: 13.4 us -> 0.02 us
  matrix products: 6.67 us -> 0 us
  local copies, waits for them, and re-layouts: 3.46 us -> 5.72 us
    reduce_scatter x1 -> x0, waiting for transfers between devices: 49.8 us -> none  [shards(): lax.psum_scatter(partial_sum.astype(BF16), 'head', scatter_dimension=1, t...]
    pallas_call x1, Pallas kernels: 76.4 us -> 113 us  [attend(): pl.pallas_call(attend_kernel, out_shape=jax.ShapeDtypeStruct((512, 1024),...]
    dot_general x1 -> x0, matrix products: 6.67 us -> none  [shards(): lax.dot_general(attended, out_weight, (((0,), (0,)), ((), ())), preferred...]
    unnamed x1 -> x2, local copies, waits for them, and re-layouts: 0.9 us -> 3.16 us
  transfers between devices with their start and end apart: 1 -> 0, of which waited for: 1 -> 0; matrix products, arithmetic and copies ran while one was open for 0% -> 0% of each run, Pallas kernels for 0% -> 0%
where the time goes in v2:
time: 120 us
  Pallas kernels  113 us (94%)
  local copies, waits for them, and re-layouts  5.72 us (5%)
  other arithmetic  1.65 us (1%)
    pallas_call x1, Pallas kernels, attend(): pl.pallas_call(attend_kernel, out_shape=jax.ShapeDtypeStruct((512, 1024),...  113 us
    unnamed x2, local copies, waits for them, and re-layouts  3.16 us

profile of v2, /device:TPU:61, one launch (start us, length us, event | category | flops | bytes accessed | tf_op | source)
XLA Modules:
  0.0 120.2 jit_solution(2393661697327220060)
XLA Ops:
  0.0 1.0 copy.7
  1.0 1.6 %pad_maximum_fusion.kv_ref = bf16[4,256,128]{2,1,0:T(8,128)(2,1)} fusion(bf16[4,128,128]{2,1,0:T(8,128)(2,1)S(1)} %bitcast.9, bf16[4,128,128]{2,1,0:T(8,128)(2,1)} %bitcast.11), kind=kLoop, calls=%fused_computation | loop fusion | flops 524288 | bytes 524288 | tf_op jit(solution)/shard_map/concatenate | solution.py:454
  2.7 1.5 %copy.6 = bf16[128,4,512]{2,1,0:T(4,128)(2,1)S(1)} copy(bf16[128,4,512]{0,1,2:T(4,128)(2,1)} %bitcast.8) | data formatting | bytes 1048576 | tf_op jit(solution)/shard_map/transpose | solution.py:451
  4.2 0.9 copy.8
  5.1 112.8 %shard_map.46 = bf16[512,1024]{1,0:T(8,128)(2,1)} custom-call(bf16[128,2048]{1,0:T(8,128)(2,1)} %bitcast.6, bf16[4,256,128]{2,1,0:T(8,128)(2,1)} %pad_maximum_fusion.kv_ref, bf16[512,4096]{1,0:T(8,128)(2,1)} %w_ref.1), custom_call_target="tpu_custom_call" | custom-call | tf_op jit(solution)/shard_map/pallas_call | solution.py:412
  117.9 2.3 %copy.10 = bf16[512,1024]{1,0:T(8,128)(2,1)} copy(bf16[512,1024]{1,0:T(8,128)(2,1)} %shard_map.46) | data formatting | bytes 2097152

commit v3 on v2

--- a/solution.py
+++ b/solution.py
@@ -12,7 +12,6 @@
 NEG = -1e30
 SCALE = 128 ** -0.5 * 1.4426950408889634
 FAR = 1 << 20
-W_LAG = 6
 PAR_STEP = 5
 TQ = 1024
 
@@ -46,7 +45,7 @@
     to_yp, to_ym, to_xp, to_xm = ctx(y + 1, x), ctx(y - 1, x), ctx(y, x + 1), ctx(y, x - 1)
 
     def slot(c, u, a):
-        return (c * 2 + u) * 16 + a
+        return (u * 16 + a) * 2 + c
 
     row = lax.broadcasted_iota(jnp.int32, (16, 128), 0)
     ones = jnp.where(row == 0, 1.0, 0.0).astype(BF16)
@@ -84,7 +83,7 @@
             src_ref=kv_ref.at[other * 2 + u],
             dst_ref=kv.at[slot(z, u, place), pl.ds(0, 256)],
             send_sem=x_send.at[u],
-            recv_sem=recv_sem.at[slot(z, u, place)],
+            recv_sem=recv_sem.at[u, place],
             device_id={"ctx": z_mate},
             device_id_type=pl.DeviceIdType.MESH,
         )
@@ -93,43 +92,31 @@
     for swap in swaps:
         swap.start()
 
-    def relay(c, u, a, target, way):
-        e = slot(c, u, a)
+    def remote(ref, sent, got, target):
         return pltpu.make_async_remote_copy(
-            src_ref=kv.at[e, pl.ds(0, 256)],
-            dst_ref=kv.at[e, pl.ds(0, 256)],
-            send_sem=send_sem.at[way, e],
-            recv_sem=recv_sem.at[e],
-            device_id={"ctx": target},
-            device_id_type=pl.DeviceIdType.MESH,
-        )
-
-    def w_rows(c, u, a):
-        return pl.ds(pl.multiple_of(((1 - zl) * 2 + u) * 512 + a * 32 + c * 16, 16), 16)
-
-    def w_relay(c, u, a, target, way):
-        e = slot(c, u, a)
+            src_ref=ref, dst_ref=ref, send_sem=sent, recv_sem=got,
+            device_id={"ctx": target}, device_id_type=pl.DeviceIdType.MESH,
+        )
+
+    def block(u, a, target, c=0, n=2):
+        return remote(kv.at[pl.ds(slot(c, u, a), n), pl.ds(0, 256)], send_sem, recv_sem.at[u, a], target)
+
+    def w_block(u, a, target, c=0, n=2):
+        rows = pl.multiple_of(((1 - zl) * 2 + u) * 512 + a * 32 + c * 16, 16)
+        return remote(w_all.at[pl.ds(rows, n * 16)], w_send, w_recv.at[u, a], target)
+
+    def w_slice(i, peer):
+        rows = place * 32
         return pltpu.make_async_remote_copy(
-            src_ref=w_all.at[w_rows(c, u, a)],
-            dst_ref=w_all.at[w_rows(c, u, a)],
-            send_sem=w_send.at[way, e],
-            recv_sem=w_recv.at[e],
-            device_id={"ctx": target},
-            device_id_type=pl.DeviceIdType.MESH,
-        )
-
-    def w_slice(c, i, peer):
-        rows = place * 32 + c * 16
-        return pltpu.make_async_remote_copy(
-            src_ref=w_ref.at[pl.ds(pl.multiple_of(rows, 16), 16), pl.ds(pl.multiple_of(peer * 1024, 1024), 1024)],
-            dst_ref=w_all.at[pl.ds(pl.multiple_of(head * 512 + rows, 16), 16)],
-            send_sem=ws_send.at[i, c],
-            recv_sem=w_recv.at[slot(c, core, place)],
+            src_ref=w_ref.at[pl.ds(pl.multiple_of(rows, 32), 32), pl.ds(pl.multiple_of(peer * 1024, 1024), 1024)],
+            dst_ref=w_all.at[pl.ds(pl.multiple_of(head * 512 + rows, 32), 32)],
+            send_sem=ws_send.at[i],
+            recv_sem=w_recv.at[core, place],
             device_id={"head": peer},
             device_id_type=pl.DeviceIdType.MESH,
         )
 
-    w_slices = [w_slice(c, i, peer) for i, peer in enumerate((far, far_twin)) for c in range(2)]
+    w_slices = [w_slice(i, peer) for i, peer in enumerate((far, far_twin))]
     w_twin = pltpu.make_async_remote_copy(
         src_ref=w_ref.at[:, pl.ds(pl.multiple_of(twin * 1024, 1024), 1024)],
         dst_ref=w_all.at[pl.ds(pl.multiple_of(head * 512, 512), 512)],
@@ -137,22 +124,40 @@
         device_id={"head": twin}, device_id_type=pl.DeviceIdType.MESH,
     )
 
-    def relays(c, u, a, first, second, act, relay=relay):
-        if u == 0:
-            p1, m1, p2, m2 = to_xp, to_xm, to_yp, to_ym
-        else:
-            p1, m1, p2, m2 = to_yp, to_ym, to_xp, to_xm
-        line = second == 0
-        conds = (
-            (line | ((second == 3) & (c == 0)), p2),
-            (line | ((second == 1) & (c == 1)), m2),
-            (line & ((first == 0) | ((first == 3) & (c == 0))), p1),
-            (line & ((first == 0) | ((first == 1) & (c == 1))), m1),
-        )
-        for way, (cond, target) in enumerate(conds):
-            @pl.when(cond)
+    ways = ((to_xp, to_xm, to_yp, to_ym), (to_yp, to_ym, to_xp, to_xm))
+
+    def pass_on(make, t):
+        second = gray(t // 4)
+        first = gray(t % 4)
+        places = [source(t, u)[0] for u in range(2)]
+        for u in range(2):
+            make(u, places[u], to_xp).wait_recv()
+
+        @pl.when(second == 0)
+        def _():
+            for u in range(2):
+                make(u, places[u], ways[u][2]).start()
+                make(u, places[u], ways[u][3]).start()
+
+            @pl.when(first == 3)
             def _():
-                act(relay(c, u, a, target, way))
+                for u in range(2):
+                    make(u, places[u], ways[u][0], 0, 1).start()
+
+            @pl.when(first == 1)
+            def _():
+                for u in range(2):
+                    make(u, places[u], ways[u][1], 1, 1).start()
+
+        @pl.when(second == 3)
+        def _():
+            for u in range(2):
+                make(u, places[u], ways[u][2], 0, 1).start()
+
+        @pl.when(second == 1)
+        def _():
+            for u in range(2):
+                make(u, places[u], ways[u][3], 1, 1).start()
 
     def source(t, u):
         second, first = gray(t // 4), gray(t % 4)
@@ -165,7 +170,8 @@
     for copy in own_copies:
         copy.wait()
     for u in range(2):
-        relays(z, u, place, 0 * place, 0 * place, lambda r: r.start())
+        for target in (to_xp, to_xm, to_yp, to_ym):
+            block(u, place, target, z, 1).start()
     swap_q = pltpu.make_async_remote_copy(
         src_ref=q_ref, dst_ref=qb.at[1], send_sem=q_sem.at[0], recv_sem=q_sem.at[1],
         device_id={"ctx": mate}, device_id_type=pl.DeviceIdType.MESH,
@@ -182,9 +188,9 @@
 
     own_q.wait()
     for u in range(2):
-        relay(other, u, place, z_mate, 0).wait_recv()
-    for u in range(2):
-        relays(other, u, place, 0 * place, 0 * place, lambda r: r.start())
+        block(u, place, z_mate, other, 1).wait_recv()
+        for target in (to_xp, to_xm, to_yp, to_ym):
+            block(u, place, target, other, 1).start()
 
     def update(n, entries, bases):
         keys = jnp.concatenate([kv[e, pl.ds(0, 128), :] for e in entries], axis=0)
@@ -261,21 +267,9 @@
         return jnp.where(n == 1, yes, no)
 
     def step(t, carry):
-        @pl.when((t > 0) & (t < 16))
-        def _():
-            for u in range(2):
-                a, first, second = source(t, u)
-                for c in range(2):
-                    relay(c, u, a, to_xp, 0).wait_recv()
-                    relays(c, u, a, first, second, lambda r: r.start())
-
-        @pl.when(t >= W_LAG)
-        def _():
-            for u in range(2):
-                a, first, second = source(t - W_LAG, u)
-                for c in range(2):
-                    w_relay(c, u, a, to_xp, 0).wait_recv()
-                    relays(c, u, a, first, second, lambda r: r.start(), w_relay)
+        @pl.when(t > 0)
+        def _():
+            pass_on(block, t)
 
         @pl.when(t == PAR_STEP)
         def _():
@@ -299,7 +293,7 @@
 
     zero = 0 * me
     start = (zero, zero) + (slot(z, 0, place),) * 7
-    own, par = lax.fori_loop(0, 16 + W_LAG, step, (start, start))
+    own, par = lax.fori_loop(0, 16, step, (start, start))
 
     def o_copy(i):
         cols = pl.ds(i * 512, 512)
@@ -317,7 +311,22 @@
     def close(j, carry):
         n = 1 - j
         state = tuple(pick(n, p, o) for o, p in zip(own, par))
-        state = lax.fori_loop(0, 16 - state[0], lambda i, st: advance(n, st), state)
+
+        def follow(i, st):
+            @pl.when((j == 1) & (i == 0))
+            def _():
+                for u in range(2):
+                    w_block(u, place, to_xp).wait_recv()
+                    for target in (to_xp, to_xm, to_yp, to_ym):
+                        w_block(u, place, target).start()
+
+            @pl.when((j == 1) & (i > 0))
+            def _():
+                pass_on(w_block, i)
+
+            return lax.fori_loop(0, jnp.where(st[0] < 16, 1, 0), lambda _, s: advance(n, s), st)
+
+        state = lax.fori_loop(0, jnp.where(j == 0, 16 - state[0], 16), follow, state)
         finish(n, state)
 
         @pl.when(j == 0)
@@ -398,13 +407,8 @@
         copy.wait_send()
     w_twin.wait_send()
 
-    @pl.loop(0, 16)
-    def _(t):
-        for u in range(2):
-            a, first, second = source(t, u)
-            for c in range(2):
-                relays(c, u, a, first, second, lambda r: r.wait_send())
-                relays(c, u, a, first, second, lambda r: r.wait_send(), w_relay)
+    remote(kv.at[pl.ds(0, 60), pl.ds(0, 256)], send_sem, recv_sem.at[0, 0], to_xp).wait_send()
+    remote(w_all.at[pl.ds(0, 960)], w_send, w_recv.at[0, 0], to_xp).wait_send()
 
 
 def attend(q_t, kv_t, weight):
@@ -426,16 +430,16 @@
             pltpu.VMEM((2048, 1024), BF16),
             pltpu.VMEM((16, 512, 128), BF16),
             pltpu.VMEM((512, 1024), F32),
-            pltpu.SemaphoreType.DMA((4, 64)),
-            pltpu.SemaphoreType.DMA((64,)),
+            pltpu.SemaphoreType.DMA,
+            pltpu.SemaphoreType.DMA((2, 16)),
             pltpu.SemaphoreType.DMA((2,)),
             pltpu.SemaphoreType.DMA((2,)),
             pltpu.SemaphoreType.DMA((2, 4)),
             pltpu.SemaphoreType.DMA((2,)),
             pltpu.SemaphoreType.DMA((4,)),
-            pltpu.SemaphoreType.DMA((4, 64)),
-            pltpu.SemaphoreType.DMA((64,)),
-            pltpu.SemaphoreType.DMA((2, 2)),
+            pltpu.SemaphoreType.DMA,
+            pltpu.SemaphoreType.DMA((2, 16)),
+            pltpu.SemaphoreType.DMA((2,)),
             pltpu.SemaphoreType.DMA,
             pltpu.SemaphoreType.DMA,
             pltpu.SemaphoreType.DMA((3, 4)),

time: 120 us -> 120 us (level)
  the two profiles are of different devices: /device:TPU:61 before, /device:TPU:1 now
where the time goes in v3:
time: 120 us; the launch traced here: 119 us
  Pallas kernels  112 us (93%)
  local copies, waits for them, and re-layouts  5.72 us (5%)
  other arithmetic  1.65 us (1%)
    pallas_call x1, Pallas kernels, attend(): pl.pallas_call(attend_kernel, out_shape=jax.ShapeDtypeStruct((512, 1024),...  112 us
    unnamed x2, local copies, waits for them, and re-layouts  3.16 us

profile of v3, /device:TPU:1, one launch (start us, length us, event | category | flops | bytes accessed | tf_op | source)
XLA Modules:
  0.0 119.3 jit_solution(2298393011130785388)
XLA Ops:
  0.0 1.0 copy.7
  1.0 1.6 %pad_maximum_fusion.kv_ref = bf16[4,256,128]{2,1,0:T(8,128)(2,1)} fusion(bf16[4,128,128]{2,1,0:T(8,128)(2,1)S(1)} %bitcast.9, bf16[4,128,128]{2,1,0:T(8,128)(2,1)} %bitcast.11), kind=kLoop, calls=%fused_computation | loop fusion | flops 524288 | bytes 524288 | tf_op jit(solution)/shard_map/concatenate | solution.py:458
  2.7 1.5 %copy.6 = bf16[128,4,512]{2,1,0:T(4,128)(2,1)S(1)} copy(bf16[128,4,512]{0,1,2:T(4,128)(2,1)} %bitcast.8) | data formatting | bytes 1048576 | tf_op jit(solution)/shard_map/transpose | solution.py:455
  4.2 0.9 copy.8
  5.1 111.9 %shard_map.46 = bf16[512,1024]{1,0:T(8,128)(2,1)} custom-call(bf16[128,2048]{1,0:T(8,128)(2,1)} %bitcast.6, bf16[4,256,128]{2,1,0:T(8,128)(2,1)} %pad_maximum_fusion.kv_ref, bf16[512,4096]{1,0:T(8,128)(2,1)} %w_ref.1), custom_call_target="tpu_custom_call" | custom-call | tf_op jit(solution)/shard_map/pallas_call | solution.py:416
  117.0 2.3 %copy.10 = bf16[512,1024]{1,0:T(8,128)(2,1)} copy(bf16[512,1024]{1,0:T(8,128)(2,1)} %shard_map.46) | data formatting | bytes 2097152

commit v4 on v3

--- a/solution.py
+++ b/solution.py
@@ -12,8 +12,7 @@
 NEG = -1e30
 SCALE = 128 ** -0.5 * 1.4426950408889634
 FAR = 1 << 20
-PAR_STEP = 5
-TQ = 1024
+TQ = 512
 
 
 def gray(n):
@@ -31,7 +30,7 @@
     place = me % 16
     other = 1 - z
     z_mate = other * 16 + place
-    mate_place = 15 - place
+    mate_place = (3 - y) * 4 + x
     mate = other * 16 + mate_place
     head = lax.axis_index("head")
     core, zl = head % 2, head // 2
@@ -39,8 +38,11 @@
     far = (1 - zl) * 2 + core
     far_twin = (1 - zl) * 2 + 1 - core
 
+    def wrap(v):
+        return jnp.where(v < 0, v + 4, jnp.where(v > 3, v - 4, v))
+
     def ctx(yy, xx):
-        return z * 16 + ((yy + 4) % 4) * 4 + (xx + 4) % 4
+        return z * 16 + wrap(yy) * 4 + wrap(xx)
 
     to_yp, to_ym, to_xp, to_xm = ctx(y + 1, x), ctx(y - 1, x), ctx(y, x + 1), ctx(y, x - 1)
 
@@ -126,10 +128,9 @@
 
     ways = ((to_xp, to_xm, to_yp, to_ym), (to_yp, to_ym, to_xp, to_xm))
 
-    def pass_on(make, t):
-        second = gray(t // 4)
-        first = gray(t % 4)
-        places = [source(t, u)[0] for u in range(2)]
+    def pass_on(make, g, e):
+        second, first = gray(g), gray(e)
+        places = (wrap(y + second) * 4 + wrap(x + first), wrap(y + first) * 4 + wrap(x + second))
         for u in range(2):
             make(u, places[u], to_xp).wait_recv()
 
@@ -158,25 +159,22 @@
         def _():
             for u in range(2):
                 make(u, places[u], ways[u][3], 1, 1).start()
-
-    def source(t, u):
-        second, first = gray(t // 4), gray(t % 4)
-        if u == 0:
-            a = ((y + second) % 4) * 4 + (x + first) % 4
-        else:
-            a = ((y + first) % 4) * 4 + (x + second) % 4
-        return a, first, second
 
     for copy in own_copies:
         copy.wait()
     for u in range(2):
         for target in (to_xp, to_xm, to_yp, to_ym):
             block(u, place, target, z, 1).start()
-    swap_q = pltpu.make_async_remote_copy(
-        src_ref=q_ref, dst_ref=qb.at[1], send_sem=q_sem.at[0], recv_sem=q_sem.at[1],
-        device_id={"ctx": mate}, device_id_type=pl.DeviceIdType.MESH,
-    )
-    swap_q.start()
+    swap_q = [
+        pltpu.make_async_remote_copy(
+            src_ref=q_ref.at[:, pl.ds(half * 1024, 1024)], dst_ref=qb.at[1, :, pl.ds(half * 1024, 1024)],
+            send_sem=q_sem.at[0, half], recv_sem=q_sem.at[1, half],
+            device_id={"ctx": mate}, device_id_type=pl.DeviceIdType.MESH,
+        )
+        for half in range(2)
+    ]
+    swap_q[0].start()
+    swap_q[1].start()
     for copy in w_slices:
         copy.start()
     w_twin.start()
@@ -192,12 +190,13 @@
         for target in (to_xp, to_xm, to_yp, to_ym):
             block(u, place, target, other, 1).start()
 
-    def update(n, entries, bases):
+    def update(n, half, entries, bases, tiles=2):
+        lanes = [pl.ds(pl.multiple_of(half * 1024 + t * TQ, TQ), TQ) for t in range(tiles)]
         keys = jnp.concatenate([kv[e, pl.ds(0, 128), :] for e in entries], axis=0)
         vals = jnp.concatenate([kv[e, pl.ds(128, 144), :] for e in entries], axis=1)
 
         def scores(t):
-            s = jnp.dot(keys, qb[n, :, pl.ds(t * TQ, TQ)], preferred_element_type=F32) * SCALE
+            s = jnp.dot(keys, qb[n, :, lanes[t]], preferred_element_type=F32) * SCALE
             if bases is not None:
                 k_at = lax.broadcasted_iota(jnp.int32, (128, TQ), 0)
                 q_at = lax.broadcasted_iota(jnp.int32, (128, TQ), 1) % 512
@@ -208,15 +207,14 @@
             return s
 
         def values(t, p, shrink):
-            rows = pl.ds(t * TQ, TQ)
+            rows = lanes[t]
             acc[n, :, rows] = acc[n, :, rows] * shrink[:1] + jnp.dot(vals, p, preferred_element_type=F32)
 
         s = scores(0)
         held = None
-        tiles = 2048 // TQ
         for t in range(tiles):
             after = scores(t + 1) if t + 1 < tiles else None
-            rows = pl.ds(t * TQ, TQ)
+            rows = lanes[t]
             before = peak[n, :, rows]
             now = jnp.maximum(before, jnp.max(s, axis=0, keepdims=True))
             p = jnp.exp2(s - now[:1]).astype(BF16)
@@ -233,67 +231,43 @@
     def at_of(n):
         return jnp.where(n == 0, place, mate_place)
 
-    def advance(n, state):
-        t, count, *held = state
-        for c in range(2):
-            for u in range(2):
-                a, _, _ = source(t, u)
-                if c == 0:
-                    ok = (kind_of(n) == 1) | (a < at_of(n))
-                else:
-                    ok = (kind_of(n) == 1) & (a < at_of(n))
-                held = [jnp.where(ok & (count == k), slot(c, u, a), r) for k, r in enumerate(held)]
-                count = count + ok.astype(jnp.int32)
-        full = count >= 4
-
-        @pl.when(full)
-        def _():
-            update(n, held[:4], None)
-
-        held = [jnp.where(full, held[k + 4] if k < 3 else r, r) for k, r in enumerate(held)]
-        return (t + 1, jnp.where(full, count - 4, count), *held)
-
-    def finish(n, state):
-        _, count, *held = state
-        entries = [slot(kind_of(n), u, at_of(n)) for u in range(2)]
-        bases = [z * 256 + u * 128 for u in range(2)]
-        for k in range(3):
-            there = k < count
-            entries.append(jnp.where(there, held[k], slot(z, 0, place)))
-            bases.append(jnp.where(there, -FAR, FAR))
-        update(n, entries, bases)
-
-    def pick(n, yes, no):
-        return jnp.where(n == 1, yes, no)
-
-    def step(t, carry):
-        @pl.when(t > 0)
-        def _():
-            pass_on(block, t)
-
-        @pl.when(t == PAR_STEP)
-        def _():
-            swap_q.wait_recv()
-
-        ready = jnp.minimum(t + 1, 16)
-
-        def one(i, carry):
-            own, par = carry
-            n = ((t >= PAR_STEP) & (par[0] < ready)).astype(jnp.int32)
-            state = advance(n, tuple(pick(n, p, o) for o, p in zip(own, par)))
-            return (
-                tuple(pick(n, o, v) for o, v in zip(own, state)),
-                tuple(pick(n, v, p) for p, v in zip(par, state)),
-            )
-
-        own, par = carry
-        open_own = ready - own[0]
-        open_par = jnp.where(t >= PAR_STEP, ready - par[0], 0)
-        return lax.fori_loop(0, jnp.minimum(open_own + open_par, 2), one, (own, par))
+    n_high = other
+
+    def early(g):
+        row, column = wrap(y + gray(g)), wrap(x + gray(g))
+        entries = [slot(0, 0, row * 4 + k) for k in range(4)] + [slot(0, 1, k * 4 + column) for k in range(4)]
+        update(n_high, 0, entries, None, 4)
+
+    def late_row(n, row):
+        return [(u, row * 4 + k) for u in range(2) for k in range(4)]
+
+    def late(n, half, row):
+        update(n, half, [slot(kind_of(n), u, a) for u, a in late_row(n, row)], None)
+
+    def diagonal(n, half, row):
+        entries, bases = [], []
+        for u, a in late_row(n, row):
+            entries.append(slot(kind_of(n), u, a))
+            bases.append(jnp.where(a < at_of(n), -FAR, jnp.where(a > at_of(n), FAR, z * 256 + u * 128)))
+        update(n, half, entries, bases)
 
     zero = 0 * me
-    start = (zero, zero) + (slot(z, 0, place),) * 7
-    own, par = lax.fori_loop(0, 16, step, (start, start))
+
+    @pl.loop(1, 4)
+    def _(e):
+        pass_on(block, zero, e)
+
+    @pl.loop(1, 4)
+    def _(g):
+        for e in range(4):
+            pass_on(block, g, zero + e)
+            if e == 1:
+                @pl.when(g == 1)
+                def _():
+                    swap_q[0].wait_recv()
+                    swap_q[1].wait_recv()
+            if e == 2:
+                early(g - 1)
 
     def o_copy(i):
         cols = pl.ds(i * 512, 512)
@@ -303,45 +277,15 @@
         )
 
     swap_o = [o_copy(i) for i in range(4)]
-    swap_st = pltpu.make_async_remote_copy(
-        src_ref=st_send, dst_ref=st_recv, send_sem=st_sem.at[0], recv_sem=st_sem.at[1],
-        device_id={"ctx": mate}, device_id_type=pl.DeviceIdType.MESH,
-    )
-
-    def close(j, carry):
-        n = 1 - j
-        state = tuple(pick(n, p, o) for o, p in zip(own, par))
-
-        def follow(i, st):
-            @pl.when((j == 1) & (i == 0))
-            def _():
-                for u in range(2):
-                    w_block(u, place, to_xp).wait_recv()
-                    for target in (to_xp, to_xm, to_yp, to_ym):
-                        w_block(u, place, target).start()
-
-            @pl.when((j == 1) & (i > 0))
-            def _():
-                pass_on(w_block, i)
-
-            return lax.fori_loop(0, jnp.where(st[0] < 16, 1, 0), lambda _, s: advance(n, s), st)
-
-        state = lax.fori_loop(0, jnp.where(j == 0, 16 - state[0], 16), follow, state)
-        finish(n, state)
-
-        @pl.when(j == 0)
-        def _():
-            st_send[pl.ds(0, 1), :] = peak[1, pl.ds(0, 1), :]
-            st_send[pl.ds(1, 1), :] = acc[1, pl.ds(128, 1), :]
-            swap_st.start()
-            for i in range(4):
-                cols = pl.ds(i * 512, 512)
-                o_send[:, cols] = acc[1, pl.ds(0, 128), cols].astype(BF16)
-                swap_o[i].start()
-
-        return carry
-
-    lax.fori_loop(0, 2, close, 0)
+
+    def st_copy(i):
+        cols = pl.ds(i * 512, 512)
+        return pltpu.make_async_remote_copy(
+            src_ref=st_send.at[:, cols], dst_ref=st_recv.at[:, cols], send_sem=st_sem.at[0, i], recv_sem=st_sem.at[1, i],
+            device_id={"ctx": mate}, device_id_type=pl.DeviceIdType.MESH,
+        )
+
+    swap_st = [st_copy(i) for i in range(4)]
 
     def att_copy(k, i, piece, peer):
         return pltpu.make_async_remote_copy(
@@ -349,58 +293,124 @@
             device_id={"head": peer}, device_id_type=pl.DeviceIdType.MESH,
         )
 
-    swap_st.wait_recv()
-    for i in range(4):
-        swap_o[i].wait_recv()
-        cols = pl.ds(i * 512, 512)
-        mine, theirs = peak[0, pl.ds(0, 1), cols], st_recv[pl.ds(0, 1), cols]
-        top = jnp.maximum(mine, theirs)
-        a0, a1 = jnp.exp2(mine - top), jnp.exp2(theirs - top)
-        norm = acc[0, pl.ds(128, 1), cols] * a0 + st_recv[pl.ds(1, 1), cols] * a1
-        mixed = acc[0, pl.ds(0, 128), cols] * a0 + o_recv[:, cols].astype(F32) * a1
-        att[head * 4 + i] = (mixed / norm).T.astype(BF16)
-        att_copy(0, i, head * 4 + i, far).start()
-        att_copy(1, i, head * 4 + i, twin).start()
-
+    def send_o(half):
+        for i in (2 * half, 2 * half + 1):
+            cols = pl.ds(i * 512, 512)
+            st_send[pl.ds(0, 1), cols] = peak[1, pl.ds(0, 1), cols]
+            st_send[pl.ds(1, 1), cols] = acc[1, pl.ds(128, 1), cols]
+            o_send[:, cols] = acc[1, pl.ds(0, 128), cols].astype(BF16)
+            swap_st[i].start()
+            swap_o[i].start()
+
+    def merge(half):
+        for i in (2 * half, 2 * half + 1):
+            swap_st[i].wait_recv()
+            swap_o[i].wait_recv()
+            cols = pl.ds(i * 512, 512)
+            mine, theirs = peak[0, pl.ds(0, 1), cols], st_recv[pl.ds(0, 1), cols]
+            top = jnp.maximum(mine, theirs)
+            a0, a1 = jnp.exp2(mine - top), jnp.exp2(theirs - top)
+            norm = acc[0, pl.ds(128, 1), cols] * a0 + st_recv[pl.ds(1, 1), cols] * a1
+            mixed = acc[0, pl.ds(0, 128), cols] * a0 + o_recv[:, cols].astype(F32) * a1
+            att[head * 4 + i] = (mixed / norm).T.astype(BF16)
+            att_copy(0, i, head * 4 + i, far).start()
+            att_copy(1, i, head * 4 + i, twin).start()
+
+    def hand_on(half):
+        for i in (2 * half, 2 * half + 1):
+            att_copy(0, i, far * 4 + i, twin).wait_recv()
+            att_copy(2, i, far * 4 + i, twin).start()
+
+    for u in range(2):
+        w_block(u, place, to_xp).wait_recv()
+        for target in (to_xp, to_xm, to_yp, to_ym):
+            w_block(u, place, target).start()
+    early(zero + 3)
+
+    def weights(w):
+        @pl.when(w < 8)
+        def _():
+            g, e = w // 2, 2 * (w % 2)
+
+            @pl.when(w > 0)
+            def _():
+                pass_on(w_block, g, e)
+
+            pass_on(w_block, g, e + 1)
+
+        return w + 1
+
+    def close(j, w):
+        n = 1 - j % 2
+        half = j // 2
+        rows = at_of(n) // 4
+
+        def follow(row, w):
+            w = weights(w)
+            late(n, half, row)
+            return w
+
+        w = lax.fori_loop(0, rows, follow, w)
+        w = weights(w)
+        diagonal(n, half, rows)
+
+        @pl.when(j == 0)
+        def _():
+            send_o(0)
+
+        @pl.when(j == 2)
+        def _():
+            send_o(1)
+            merge(0)
+
+        return w
+
+    w_done = lax.fori_loop(0, 4, close, zero)
+    lax.fori_loop(0, 8 - w_done, lambda i, w: weights(w), w_done)
+
+    merge(1)
+    hand_on(0)
     own_w.wait()
     w_twin.wait_recv()
 
-    def project(g, carry):
+    def project(k, carry):
+        half, g = k // 4, k % 4
         h = jnp.where(g == 0, head, jnp.where(g == 1, twin, jnp.where(g == 2, far, far_twin)))
 
-        @pl.when(g > 0)
-        def _():
-            for i in range(4):
-                att_copy(0, i, h * 4 + i, twin).wait_recv()
-
-                @pl.when(g == 2)
-                def _():
-                    att_copy(2, i, h * 4 + i, twin).start()
-
-        left = jnp.concatenate([att[h * 4 + i] for i in range(4)], axis=1)
-        right = w_all[pl.ds(pl.multiple_of(h * 512, 512), 512), :]
+        @pl.when((g == 1) | (g == 3))
+        def _():
+            for i in range(2):
+                att_copy(0, 0, h * 4 + half * 2 + i, twin).wait_recv()
+
+        @pl.when((g == 2) & (half == 1))
+        def _():
+            hand_on(1)
+
+        left = jnp.concatenate([att[h * 4 + half * 2 + i] for i in range(2)], axis=1)
+        right = w_all[pl.ds(pl.multiple_of(h * 512 + half * 256, 256), 256), :]
         term = jnp.dot(left, right, preferred_element_type=F32)
 
-        @pl.when(g == 0)
+        @pl.when(k == 0)
         def _():
             total[...] = term
 
-        @pl.when(g > 0)
+        @pl.when(k > 0)
         def _():
             total[...] += term
 
         return carry
 
-    lax.fori_loop(0, 4, project, 0)
+    lax.fori_loop(0, 8, project, 0)
     out_ref[...] = total[...].astype(BF16)
 
-    swap_st.wait_send()
     for i in range(4):
+        swap_st[i].wait_send()
         swap_o[i].wait_send()
         att_copy(0, i, head * 4 + i, far).wait_send()
         att_copy(1, i, head * 4 + i, twin).wait_send()
         att_copy(2, i, far * 4 + i, twin).wait_send()
-    swap_q.wait_send()
+    for swap in swap_q:
+        swap.wait_send()
     for swap in swaps:
         swap.wait_send()
     for copy in w_slices:
@@ -433,9 +443,9 @@
             pltpu.SemaphoreType.DMA,
             pltpu.SemaphoreType.DMA((2, 16)),
             pltpu.SemaphoreType.DMA((2,)),
-            pltpu.SemaphoreType.DMA((2,)),
+            pltpu.SemaphoreType.DMA((2, 2)),
             pltpu.SemaphoreType.DMA((2, 4)),
-            pltpu.SemaphoreType.DMA((2,)),
+            pltpu.SemaphoreType.DMA((2, 4)),
             pltpu.SemaphoreType.DMA((4,)),
             pltpu.SemaphoreType.DMA,
             pltpu.SemaphoreType.DMA((2, 16)),

time: 120 us -> 106 us (0.88)
  Pallas kernels: 112 us -> 98.2 us
    pallas_call x1, Pallas kernels: 112 us -> 98.2 us  [attend(): pl.pallas_call(attend_kernel, out_shape=jax.ShapeDtypeStruct((512, 1024),...]
where the time goes in v4:
time: 106 us
  Pallas kernels  98.2 us (93%)
  local copies, waits for them, and re-layouts  5.72 us (5%)
  other arithmetic  1.65 us (2%)
    pallas_call x1, Pallas kernels, attend(): pl.pallas_call(attend_kernel, out_shape=jax.ShapeDtypeStruct((512, 1024),...  98.2 us
    unnamed x2, local copies, waits for them, and re-layouts  3.16 us

profile of v4, /device:TPU:1, one launch (start us, length us, event | category | flops | bytes accessed | tf_op | source)
XLA Modules:
  0.0 105.6 jit_solution(16048379077045078183)
XLA Ops:
  0.0 1.0 copy.7
  1.0 1.6 %pad_maximum_fusion.kv_ref = bf16[4,256,128]{2,1,0:T(8,128)(2,1)} fusion(bf16[4,128,128]{2,1,0:T(8,128)(2,1)S(1)} %bitcast.9, bf16[4,128,128]{2,1,0:T(8,128)(2,1)} %bitcast.11), kind=kLoop, calls=%fused_computation | loop fusion | flops 524288 | bytes 524288 | tf_op jit(solution)/shard_map/concatenate | solution.py:468
  2.7 1.5 %copy.6 = bf16[128,4,512]{2,1,0:T(4,128)(2,1)S(1)} copy(bf16[128,4,512]{0,1,2:T(4,128)(2,1)} %bitcast.8) | data formatting | bytes 1048576 | tf_op jit(solution)/shard_map/transpose | solution.py:465
  4.2 0.9 copy.8
  5.1 98.2 %shard_map.46 = bf16[512,1024]{1,0:T(8,128)(2,1)} custom-call(bf16[128,2048]{1,0:T(8,128)(2,1)} %bitcast.6, bf16[4,256,128]{2,1,0:T(8,128)(2,1)} %pad_maximum_fusion.kv_ref, bf16[512,4096]{1,0:T(8,128)(2,1)} %w_ref.1), custom_call_target="tpu_custom_call" | custom-call | tf_op jit(solution)/shard_map/pallas_call | solution.py:426
  103.3 2.3 %copy.10 = bf16[512,1024]{1,0:T(8,128)(2,1)} copy(bf16[512,1024]{1,0:T(8,128)(2,1)} %shard_map.46) | data formatting | bytes 2097152

commit v5 on v4

--- a/solution.py
+++ b/solution.py
@@ -23,14 +23,14 @@
     q_ref, kv_ref, w_ref, out_ref,
     kv, qb, acc, peak, o_send, o_recv, st_send, st_recv, w_all, att, total,
     send_sem, recv_sem, x_send, q_sem, o_sem, st_sem, local_sem,
-    w_send, w_recv, ws_send, wm_send, wm_recv, att_send, att_recv,
+    w_send, w_recv, wd_recv, ws_send, wm_send, wm_recv, att_send, att_recv,
 ):
     me = lax.axis_index("ctx")
     z, y, x = me // 16, (me // 4) % 4, me % 4
     place = me % 16
     other = 1 - z
     z_mate = other * 16 + place
-    mate_place = (3 - y) * 4 + x
+    mate_place = place
     mate = other * 16 + mate_place
     head = lax.axis_index("head")
     core, zl = head % 2, head // 2
@@ -104,21 +104,21 @@
         return remote(kv.at[pl.ds(slot(c, u, a), n), pl.ds(0, 256)], send_sem, recv_sem.at[u, a], target)
 
     def w_block(u, a, target, c=0, n=2):
-        rows = pl.multiple_of(((1 - zl) * 2 + u) * 512 + a * 32 + c * 16, 16)
-        return remote(w_all.at[pl.ds(rows, n * 16)], w_send, w_recv.at[u, a], target)
-
-    def w_slice(i, peer):
-        rows = place * 32
+        rows = pl.multiple_of(((1 - zl) * 2 + u) * 512 + a * 16, 16)
+        return remote(w_all.at[pl.ds(rows, 16), pl.ds(c * 512, n * 512)], w_send, w_recv.at[u, a], target)
+
+    def w_slice(i, peer, first, rows, got):
         return pltpu.make_async_remote_copy(
-            src_ref=w_ref.at[pl.ds(pl.multiple_of(rows, 32), 32), pl.ds(pl.multiple_of(peer * 1024, 1024), 1024)],
-            dst_ref=w_all.at[pl.ds(pl.multiple_of(head * 512 + rows, 32), 32)],
+            src_ref=w_ref.at[pl.ds(pl.multiple_of(first, 16), rows), pl.ds(pl.multiple_of(peer * 1024, 1024), 1024)],
+            dst_ref=w_all.at[pl.ds(pl.multiple_of(head * 512 + first, 16), rows)],
             send_sem=ws_send.at[i],
-            recv_sem=w_recv.at[core, place],
+            recv_sem=got,
             device_id={"head": peer},
             device_id_type=pl.DeviceIdType.MESH,
         )
 
-    w_slices = [w_slice(i, peer) for i, peer in enumerate((far, far_twin))]
+    w_slices = [w_slice(i, peer, place * 16, 16, w_recv.at[core, place]) for i, peer in enumerate((far, far_twin))]
+    w_direct = [w_slice(2 + i, peer, 256, 256, wd_recv.at[core]) for i, peer in enumerate((far, far_twin))]
     w_twin = pltpu.make_async_remote_copy(
         src_ref=w_ref.at[:, pl.ds(pl.multiple_of(twin * 1024, 1024), 1024)],
         dst_ref=w_all.at[pl.ds(pl.multiple_of(head * 512, 512), 512)],
@@ -175,7 +175,7 @@
     ]
     swap_q[0].start()
     swap_q[1].start()
-    for copy in w_slices:
+    for copy in w_slices + w_direct:
         copy.start()
     w_twin.start()
 
@@ -372,6 +372,8 @@
     hand_on(0)
     own_w.wait()
     w_twin.wait_recv()
+    for i in range(2):
+        w_slice(2, far, 256, 256, wd_recv.at[i]).wait_recv()
 
     def project(k, carry):
         half, g = k // 4, k % 4
@@ -413,12 +415,12 @@
         swap.wait_send()
     for swap in swaps:
         swap.wait_send()
-    for copy in w_slices:
+    for copy in w_slices + w_direct:
         copy.wait_send()
     w_twin.wait_send()
 
     remote(kv.at[pl.ds(0, 60), pl.ds(0, 256)], send_sem, recv_sem.at[0, 0], to_xp).wait_send()
-    remote(w_all.at[pl.ds(0, 960)], w_send, w_recv.at[0, 0], to_xp).wait_send()
+    remote(w_all.at[pl.ds(0, 480)], w_send, w_recv.at[0, 0], to_xp).wait_send()
 
 
 def attend(q_t, kv_t, weight):
@@ -450,6 +452,7 @@
             pltpu.SemaphoreType.DMA,
             pltpu.SemaphoreType.DMA((2, 16)),
             pltpu.SemaphoreType.DMA((2,)),
+            pltpu.SemaphoreType.DMA((4,)),
             pltpu.SemaphoreType.DMA,
             pltpu.SemaphoreType.DMA,
             pltpu.SemaphoreType.DMA((3, 4)),

time: 106 us -> 95 us (0.90)
  the two profiles are of different devices: /device:TPU:1 before, /device:TPU:61 now
where the time goes in v5:
time: 95 us; the launch traced here: 94 us
  Pallas kernels  86.6 us (91%)
  local copies, waits for them, and re-layouts  5.72 us (6%)
  other arithmetic  1.65 us (2%)
    pallas_call x1, Pallas kernels, attend(): pl.pallas_call(attend_kernel, out_shape=jax.ShapeDtypeStruct((512, 1024),...  86.6 us
    unnamed x2, local copies, waits for them, and re-layouts  3.16 us

profile of v5, /device:TPU:61, one launch (start us, length us, event | category | flops | bytes accessed | tf_op | source)
XLA Modules:
  0.0 94.0 jit_solution(10626576585228417101)
XLA Ops:
  0.0 1.0 %copy.7 = bf16[4,128,128]{1,2,0:T(8,128)(2,1)S(1)} copy(bf16[4,128,128]{2,1,0:T(8,128)(2,1)} %bitcast.10) | data formatting | bytes 262144 | tf_op jit(solution)/shard_map/reshape | solution.py:470
  1.0 1.6 %pad_maximum_fusion.kv_ref = bf16[4,256,128]{2,1,0:T(8,128)(2,1)} fusion(bf16[4,128,128]{2,1,0:T(8,128)(2,1)S(1)} %bitcast.9, bf16[4,128,128]{2,1,0:T(8,128)(2,1)} %bitcast.11), kind=kLoop, calls=%fused_computation | loop fusion | flops 524288 | bytes 524288 | tf_op jit(solution)/shard_map/concatenate | solution.py:471
  2.7 1.5 %copy.6 = bf16[128,4,512]{2,1,0:T(4,128)(2,1)S(1)} copy(bf16[128,4,512]{0,1,2:T(4,128)(2,1)} %bitcast.8) | data formatting | bytes 1048576 | tf_op jit(solution)/shard_map/transpose | solution.py:468
  4.2 0.9 copy.8
  5.1 86.6 %shard_map.46 = bf16[512,1024]{1,0:T(8,128)(2,1)} custom-call(bf16[128,2048]{1,0:T(8,128)(2,1)} %bitcast.6, bf16[4,256,128]{2,1,0:T(8,128)(2,1)} %pad_maximum_fusion.kv_ref, bf16[512,4096]{1,0:T(8,128)(2,1)} %w_ref.1), custom_call_target="tpu_custom_call" | custom-call | tf_op jit(solution)/shard_map/pallas_call | solution.py:428
  91.8 2.3 %copy.10 = bf16[512,1024]{1,0:T(8,128)(2,1)} copy(bf16[512,1024]{1,0:T(8,128)(2,1)} %shard_map.46) | data formatting | bytes 2097152

commit v6 on v5

--- a/solution.py
+++ b/solution.py
@@ -20,8 +20,8 @@
 
 
 def attend_kernel(
-    q_ref, kv_ref, w_ref, out_ref,
-    kv, qb, acc, peak, o_send, o_recv, st_send, st_recv, w_all, att, total,
+    q_ref, k_ref, v_ref, w_ref, out_ref,
+    swap_kv,    kv, qb, acc, peak, o_send, o_recv, st_send, st_recv, w_all, att, total,
     send_sem, recv_sem, x_send, q_sem, o_sem, st_sem, local_sem,
     w_send, w_recv, wd_recv, ws_send, wm_send, wm_recv, att_send, att_recv,
 ):
@@ -56,16 +56,6 @@
     def _(e):
         kv[e, pl.ds(256, 16), :] = ones
 
-    own_copies = [
-        pltpu.make_async_copy(
-            kv_ref.at[z * 2 + u], kv.at[slot(z, u, place), pl.ds(0, 256)], local_sem.at[u]
-        )
-        for u in range(2)
-    ]
-    own_q = pltpu.make_async_copy(q_ref, qb.at[0], local_sem.at[2])
-    for copy in own_copies:
-        copy.start()
-    own_q.start()
     own_w = pltpu.make_async_copy(
         w_ref.at[:, pl.ds(pl.multiple_of(head * 1024, 1024), 1024)],
         w_all.at[pl.ds(pl.multiple_of(head * 512, 512), 512)],
@@ -73,6 +63,14 @@
     )
     own_w.start()
 
+    for u in range(2):
+        for target, part in ((kv.at[slot(z, u, place)], z * 2 + u), (swap_kv.at[u], other * 2 + u)):
+            rows = pl.ds(pl.multiple_of(part * 128, 128), 128)
+            target[pl.ds(0, 128), :] = k_ref[rows, :]
+            target[pl.ds(128, 128), :] = v_ref[rows, :].T
+    for h in range(4):
+        qb[0, :, pl.ds(h * 512, 512)] = q_ref[:, pl.ds(h * 128, 128)].T
+
     barrier = pltpu.get_barrier_semaphore()
     for peer in (to_yp, to_ym, to_xp, to_xm, z_mate, mate):
         pl.semaphore_signal(barrier, inc=1, device_id={"ctx": peer}, device_id_type=pl.DeviceIdType.MESH)
@@ -82,7 +80,7 @@
 
     swaps = [
         pltpu.make_async_remote_copy(
-            src_ref=kv_ref.at[other * 2 + u],
+            src_ref=swap_kv.at[u],
             dst_ref=kv.at[slot(z, u, place), pl.ds(0, 256)],
             send_sem=x_send.at[u],
             recv_sem=recv_sem.at[u, place],
@@ -160,14 +158,12 @@
             for u in range(2):
                 make(u, places[u], ways[u][3], 1, 1).start()
 
-    for copy in own_copies:
-        copy.wait()
     for u in range(2):
         for target in (to_xp, to_xm, to_yp, to_ym):
             block(u, place, target, z, 1).start()
     swap_q = [
         pltpu.make_async_remote_copy(
-            src_ref=q_ref.at[:, pl.ds(half * 1024, 1024)], dst_ref=qb.at[1, :, pl.ds(half * 1024, 1024)],
+            src_ref=qb.at[0, :, pl.ds(half * 1024, 1024)], dst_ref=qb.at[1, :, pl.ds(half * 1024, 1024)],
             send_sem=q_sem.at[0, half], recv_sem=q_sem.at[1, half],
             device_id={"ctx": mate}, device_id_type=pl.DeviceIdType.MESH,
         )
@@ -184,7 +180,6 @@
         acc[n] = jnp.zeros(acc.shape[1:], F32)
         peak[n] = jnp.full(peak.shape[1:], NEG, F32)
 
-    own_q.wait()
     for u in range(2):
         block(u, place, z_mate, other, 1).wait_recv()
         for target in (to_xp, to_xm, to_yp, to_ym):
@@ -251,11 +246,29 @@
             bases.append(jnp.where(a < at_of(n), -FAR, jnp.where(a > at_of(n), FAR, z * 256 + u * 128)))
         update(n, half, entries, bases)
 
+    def ahead_row(g):
+        row = wrap(y + gray(g))
+        return row, row < y
+
+    def late_ahead(g):
+        row, seen = ahead_row(g)
+
+        @pl.when(seen)
+        def _():
+            for n in range(2):
+                update(n, 0, [slot(kind_of(n), 0, row * 4 + k) for k in range(4)], None, 4)
+
+    def late_rest(n, half, row):
+        update(n, half, [slot(kind_of(n), 1, row * 4 + k) for k in range(4)], None)
+
     zero = 0 * me
 
     @pl.loop(1, 4)
     def _(e):
         pass_on(block, zero, e)
+
+    def late_loop():
+        lax.fori_loop(1, 3, lambda g, c: late_ahead(g), None)
 
     @pl.loop(1, 4)
     def _(g):
@@ -268,6 +281,10 @@
                     swap_q[1].wait_recv()
             if e == 2:
                 early(g - 1)
+            if e == 0:
+                @pl.when(g == 3)
+                def _():
+                    late_loop()
 
     def o_copy(i):
         cols = pl.ds(i * 512, 512)
@@ -347,7 +364,16 @@
 
         def follow(row, w):
             w = weights(w)
-            late(n, half, row)
+            done = (row == y - 1) | ((y == 3) & (row == 0))
+
+            @pl.when(done)
+            def _():
+                late_rest(n, half, row)
+
+            @pl.when(jnp.logical_not(done))
+            def _():
+                late(n, half, row)
+
             return w
 
         w = lax.fori_loop(0, rows, follow, w)
@@ -423,14 +449,15 @@
     remote(w_all.at[pl.ds(0, 480)], w_send, w_recv.at[0, 0], to_xp).wait_send()
 
 
-def attend(q_t, kv_t, weight):
+def attend(queries, keys, values, weight):
     vmem = pl.BlockSpec(memory_space=pltpu.VMEM)
     return pl.pallas_call(
         attend_kernel,
         out_shape=jax.ShapeDtypeStruct((512, 1024), BF16),
-        in_specs=[vmem, vmem, pl.BlockSpec(memory_space=pl.ANY)],
+        in_specs=[vmem, vmem, vmem, pl.BlockSpec(memory_space=pl.ANY)],
         out_specs=vmem,
         scratch_shapes=[
+            pltpu.VMEM((2, 256, 128), BF16),
             pltpu.VMEM((64, 272, 128), BF16),
             pltpu.VMEM((2, 128, 2048), BF16),
             pltpu.VMEM((2, 144, 2048), F32),
@@ -461,15 +488,14 @@
         compiler_params=pltpu.CompilerParams(
             collective_id=0, has_side_effects=True, vmem_limit_bytes=56 * 2 ** 20
         ),
-    )(q_t, kv_t, weight)
+    )(queries, keys, values, weight)
 
 
 def shards(queries, keys, values, out_weight):
-    q_t = queries.transpose(2, 1, 0).reshape(128, 2048)
-    k_t = keys.reshape(4, 128, 128)
-    v_t = values.reshape(4, 128, 128).transpose(0, 2, 1)
-    kv_t = jnp.concatenate([k_t, v_t], axis=1)
-    return attend(q_t, kv_t, out_weight)
+    rows = queries.shape[0]
+    return attend(
+        queries.reshape(rows, 512), keys.reshape(rows, 128), values.reshape(rows, 128), out_weight
+    )
 
 
 def solution(mesh):

time: 95 us -> 91 us (0.958)
  other arithmetic: 1.65 us -> 0 us
  local copies, waits for them, and re-layouts: 5.72 us -> 4.18 us
  Pallas kernels: 86.6 us -> 85.2 us
    concatenate x1 -> x0, other arithmetic: 1.65 us -> none  [shards(): kv_t = jnp.concatenate([k_t, v_t], axis=1)]
    transpose x1 -> x0, local copies, waits for them, and re-layouts: 1.54 us -> none  [shards(): q_t = queries.transpose(2, 1, 0).reshape(128, 2048)]
    pallas_call x1, Pallas kernels: 86.6 us -> 85.2 us  [attend(): pl.pallas_call(attend_kernel, out_shape=jax.ShapeDtypeStruct((512, 1024),...]
    reshape x1 -> x0, local copies, waits for them, and re-layouts: 1.02 us -> none  [shards(): v_t = values.reshape(4, 128, 128).transpose(0, 2, 1)]
    unnamed x2, local copies, waits for them, and re-layouts: 3.16 us -> 4.18 us
where the time goes in v6:
time: 91 us; the launch traced here: 89.4 us
  Pallas kernels  85.2 us (94%)
  local copies, waits for them, and re-layouts  4.18 us (5%)
    pallas_call x1, Pallas kernels, attend(): pl.pallas_call(attend_kernel, out_shape=jax.ShapeDtypeStruct((512, 1024),...  85.2 us
    unnamed x2, local copies, waits for them, and re-layouts  4.18 us

profile of v6, /device:TPU:61, one launch (start us, length us, event | category | flops | bytes accessed | tf_op | source)
XLA Modules:
  0.0 89.4 jit_solution(14371579321131693767)
XLA Ops:
  0.0 1.9 %copy.7 = bf16[64,8,4,128]{3,1,2,0:T(8,128)(2,1)} copy(bf16[64,8,4,128]{3,2,1,0:T(4,128)(2,1)} %bitcast.7) | data formatting | bytes 1048576
  1.9 85.2 %shard_map.46 = bf16[512,1024]{1,0:T(8,128)(2,1)} custom-call(bf16[512,512]{1,0:T(8,128)(2,1)} %bitcast.6, bf16[512,128]{1,0:T(8,128)(2,1)} %bitcast.8, bf16[512,128]{1,0:T(8,128)(2,1)} %bitcast.9, bf16[512,4096]{1,0:T(8,128)(2,1)} %w_ref.1), custom_call_target="tpu_custom_call" | custom-call | tf_op jit(solution)/shard_map/pallas_call | solution.py:454
  87.1 2.3 %copy.9 = bf16[512,1024]{1,0:T(8,128)(2,1)} copy(bf16[512,1024]{1,0:T(8,128)(2,1)} %shard_map.46) | data formatting | bytes 2097152

commit v7 on v6

--- a/solution.py
+++ b/solution.py
@@ -236,15 +236,15 @@
     def late_row(n, row):
         return [(u, row * 4 + k) for u in range(2) for k in range(4)]
 
-    def late(n, half, row):
-        update(n, half, [slot(kind_of(n), u, a) for u, a in late_row(n, row)], None)
-
-    def diagonal(n, half, row):
+    def late(n, half, row, tiles):
+        update(n, half, [slot(kind_of(n), u, a) for u, a in late_row(n, row)], None, tiles)
+
+    def diagonal(n, half, row, tiles):
         entries, bases = [], []
         for u, a in late_row(n, row):
             entries.append(slot(kind_of(n), u, a))
             bases.append(jnp.where(a < at_of(n), -FAR, jnp.where(a > at_of(n), FAR, z * 256 + u * 128)))
-        update(n, half, entries, bases)
+        update(n, half, entries, bases, tiles)
 
     def ahead_row(g):
         row = wrap(y + gray(g))
@@ -258,8 +258,8 @@
             for n in range(2):
                 update(n, 0, [slot(kind_of(n), 0, row * 4 + k) for k in range(4)], None, 4)
 
-    def late_rest(n, half, row):
-        update(n, half, [slot(kind_of(n), 1, row * 4 + k) for k in range(4)], None)
+    def late_rest(n, half, row, tiles):
+        update(n, half, [slot(kind_of(n), 1, row * 4 + k) for k in range(4)], None, tiles)
 
     zero = 0 * me
 
@@ -357,41 +357,40 @@
 
         return w + 1
 
-    def close(j, w):
-        n = 1 - j % 2
-        half = j // 2
-        rows = at_of(n) // 4
-
+    def close(n, half, w, tiles):
         def follow(row, w):
             w = weights(w)
             done = (row == y - 1) | ((y == 3) & (row == 0))
 
             @pl.when(done)
             def _():
-                late_rest(n, half, row)
+                late_rest(n, half, row, tiles)
 
             @pl.when(jnp.logical_not(done))
             def _():
-                late(n, half, row)
+                late(n, half, row, tiles)
 
             return w
 
-        w = lax.fori_loop(0, rows, follow, w)
+        w = lax.fori_loop(0, y, follow, w)
         w = weights(w)
-        diagonal(n, half, rows)
-
-        @pl.when(j == 0)
-        def _():
-            send_o(0)
-
-        @pl.when(j == 2)
-        def _():
-            send_o(1)
+        diagonal(n, half, y, tiles)
+        return w
+
+    w_par = close(1, 0, zero, 4)
+    send_o(0)
+    send_o(1)
+
+    def close_own(half, w):
+        w = close(0, half, w, 2)
+
+        @pl.when(half == 0)
+        def _():
             merge(0)
 
         return w
 
-    w_done = lax.fori_loop(0, 4, close, zero)
+    w_done = lax.fori_loop(0, 2, close_own, w_par)
     lax.fori_loop(0, 8 - w_done, lambda i, w: weights(w), w_done)
 
     merge(1)

time: 91 us -> 89.5 us (0.984)
  Pallas kernels: 85.2 us -> 83.8 us
    pallas_call x1, Pallas kernels: 85.2 us -> 83.8 us  [attend(): pl.pallas_call(attend_kernel, out_shape=jax.ShapeDtypeStruct((512, 1024),...]
where the time goes in v7:
time: 89.5 us; the launch traced here: 87.9 us
  Pallas kernels  83.8 us (94%)
  local copies, waits for them, and re-layouts  4.18 us (5%)
    pallas_call x1, Pallas kernels, attend(): pl.pallas_call(attend_kernel, out_shape=jax.ShapeDtypeStruct((512, 1024),...  83.8 us
    unnamed x2, local copies, waits for them, and re-layouts  4.18 us

profile of v7, /device:TPU:61, one launch (start us, length us, event | category | flops | bytes accessed | tf_op | source)
XLA Modules:
  0.0 87.9 jit_solution(5687725653856663324)
XLA Ops:
  0.0 1.9 %copy.7 = bf16[64,8,4,128]{3,1,2,0:T(8,128)(2,1)} copy(bf16[64,8,4,128]{3,2,1,0:T(4,128)(2,1)} %bitcast.7) | data formatting | bytes 1048576
  1.9 83.8 %shard_map.46 = bf16[512,1024]{1,0:T(8,128)(2,1)} custom-call(bf16[512,512]{1,0:T(8,128)(2,1)} %bitcast.6, bf16[512,128]{1,0:T(8,128)(2,1)} %bitcast.8, bf16[512,128]{1,0:T(8,128)(2,1)} %bitcast.9, bf16[512,4096]{1,0:T(8,128)(2,1)} %w_ref.1), custom_call_target="tpu_custom_call" | custom-call | tf_op jit(solution)/shard_map/pallas_call | solution.py:453
  85.7 2.3 %copy.9 = bf16[512,1024]{1,0:T(8,128)(2,1)} copy(bf16[512,1024]{1,0:T(8,128)(2,1)} %shard_map.46) | data formatting | bytes 2097152
